TPU v7x, 768 devices: a whole 4x8x12 slice. The times are simulated.
768 devices in a mesh: seq: 96 (over x, y, z_lo), head: 8 (over z_hi, core).
Axes of the slice: x: 4, y: 8, z: 12 (z_hi: 4, z_lo: 3; z = z_hi * 3 + z_lo), core: 2. Of those that a mesh axis runs over, the one named last changes fastest.
Arguments:
- query_heads: bfloat16 [12288, 3072], P('seq', 'head'), may hold values from -6 to 6
- key_heads: bfloat16 [12288, 1024], P('seq', 'head'), may hold values from -6 to 6
- value_heads: bfloat16 [12288, 1024], P('seq', 'head'), may hold values from -6 to 6
- out_weight: bfloat16 [3072, 3072], P('head'), may hold values from -0.109375 to 0.109375
- out_grad: bfloat16 [12288, 3072], P('seq', 'head'), may hold values from -6 to 6
- clip_lengths: int32 [8], replicated, may hold values from 1 to 3072, 12288 in all
Outputs:
- mixed: bfloat16 [12288, 3072], P('seq', 'head')
- attended: bfloat16 [12288, 3072], P('seq', 'head')
- d_queries: bfloat16 [12288, 3072], P('seq', 'head')
- d_keys: bfloat16 [12288, 1024], P('seq', 'head')
- d_values: bfloat16 [12288, 1024], P('seq', 'head')
Inputs may be any that keep to these rules, and one draw needn't show every extreme that they name: `clip_lengths`: the longest clip has exactly 3072 tokens and all sum to 12288.
All inputs are finite; a program needn't handle non-finite values.
Results may differ from a plain program's by a relative error of at most 0.03.
Values may be sent and summed in bfloat16 or wider, within the bound.
A program may use at most 32 MiB of HBM per device.

v0:
```python
import math

import jax
import jax.numpy as jnp
from jax import lax
from jax.sharding import PartitionSpec as P

HEADS = 24
KV_HEADS = 8
HD = 128


def from_behind(value, axis, steps):
    count = lax.axis_size(axis)
    first, last = (max(0, -steps), min(count, count - steps))
    return lax.ppermute(value, axis, [(source, source + steps) for source in range(first, last)])


def clip_index(positions, clip_lengths):
    clip_ends = jnp.cumsum(clip_lengths)
    return jnp.sum((positions[:, None] >= clip_ends[None, :]).astype(jnp.int32), axis=1)


def shards(query_heads, key_heads, value_heads, out_weight, out_grad, clip_lengths):
    tok_rows = query_heads.shape[0]
    kv_local = key_heads.shape[1] // HD
    group_size = HEADS // KV_HEADS
    seq_count = lax.axis_size("seq")
    span_devices = min(24, seq_count // 2)
    seq_index = lax.axis_index("seq")
    score_scale = 1.0 / math.sqrt(HD)
    key_width = (span_devices + 1) * tok_rows
    kv_pair = jnp.stack([key_heads, value_heads])
    stored_first = jnp.zeros((span_devices + 1,) + kv_pair.shape, kv_pair.dtype).at[0].set(kv_pair)

    def collect(step_num, loop_state):
        stored, moving = loop_state
        moving = from_behind(moving, "seq", 1)
        stored = lax.dynamic_update_index_in_dim(stored, moving, step_num, 0)
        return (stored, moving)

    stored, _ = lax.fori_loop(1, span_devices + 1, collect, (stored_first, kv_pair))
    distance = jnp.arange(span_devices + 1, dtype=jnp.int32)
    source = (seq_index - distance) % seq_count
    key_pos = (source[:, None] * tok_rows + jnp.arange(tok_rows, dtype=jnp.int32)[None, :]).reshape(
        -1
    )
    query_pos = seq_index * tok_rows + jnp.arange(tok_rows, dtype=jnp.int32)
    allowed = (
        clip_index(query_pos, clip_lengths)[:, None] == clip_index(key_pos, clip_lengths)[None, :]
    ) & (key_pos[None, :] <= query_pos[:, None])
    key_all = stored[:, 0].reshape(key_width, kv_local, HD)
    value_all = stored[:, 1].reshape(key_width, kv_local, HD)
    query_grid = query_heads.reshape(tok_rows, kv_local, group_size, HD)
    scores = (
        jnp.einsum("tgcd,sgd->gcts", query_grid, key_all, preferred_element_type=jnp.float32)
        * score_scale
    )
    scores = jnp.where(allowed, scores, -1e30)
    row_max = jnp.max(scores, axis=-1, keepdims=True)
    row_total = jnp.sum(jnp.exp(scores - row_max), axis=-1, keepdims=True)
    probabilities = jnp.exp(scores - (row_max + jnp.log(row_total)))
    weights = probabilities.astype(jnp.bfloat16)
    attended_grid = jnp.einsum(
        "gcts,sgd->tgcd", weights, value_all, preferred_element_type=jnp.float32
    ).astype(jnp.bfloat16)
    attended = attended_grid.reshape(tok_rows, -1)
    partial_value = jnp.dot(attended, out_weight, preferred_element_type=jnp.float32)
    mixed = lax.psum_scatter(
        partial_value.astype(jnp.bfloat16), "head", scatter_dimension=1, tiled=True
    )
    d_heads = lax.dot_general(
        lax.all_gather(out_grad, "head", axis=1, tiled=True),
        out_weight,
        (((1,), (1,)), ((), ())),
        preferred_element_type=jnp.float32,
    ).astype(jnp.bfloat16)
    grad_grid = d_heads.reshape(tok_rows, kv_local, group_size, HD)
    row_delta = jnp.sum(grad_grid.astype(jnp.float32) * attended_grid.astype(jnp.float32), axis=-1)
    row_delta = jnp.transpose(row_delta, (1, 2, 0))[..., None]
    dprob = jnp.einsum("tgcd,sgd->gcts", grad_grid, value_all, preferred_element_type=jnp.float32)
    dscores = (probabilities * (dprob - row_delta)).astype(jnp.bfloat16)
    d_queries = (
        (
            jnp.einsum("gcts,sgd->tgcd", dscores, key_all, preferred_element_type=jnp.float32)
            * score_scale
        )
        .astype(jnp.bfloat16)
        .reshape(tok_rows, -1)
    )
    dkey_all = (
        jnp.einsum("gcts,tgcd->sgd", dscores, query_grid, preferred_element_type=jnp.float32)
        * score_scale
    )
    dvalue_all = jnp.einsum(
        "gcts,tgcd->sgd", weights, grad_grid, preferred_element_type=jnp.float32
    )
    gradients = jnp.stack(
        [
            dkey_all.reshape(span_devices + 1, tok_rows, -1),
            dvalue_all.reshape(span_devices + 1, tok_rows, -1),
        ],
        axis=1,
    )

    def carry_against(step_num, collected):
        collected = collected + lax.dynamic_index_in_dim(
            gradients, span_devices - step_num, 0, keepdims=False
        )
        return from_behind(collected.astype(jnp.bfloat16), "seq", -1).astype(collected.dtype)

    collected = lax.fori_loop(
        0, span_devices, carry_against, jnp.zeros(gradients.shape[1:], jnp.float32)
    )
    finished = collected + gradients[0]
    d_keys = finished[0].astype(jnp.bfloat16)
    d_values = finished[1].astype(jnp.bfloat16)
    return (mixed, attended, d_queries, d_keys, d_values)


def solution(mesh):
    in_specs = (
        P("seq", "head"),
        P("seq", "head"),
        P("seq", "head"),
        P("head", None),
        P("seq", "head"),
        P(),
    )
    out_specs = (
        P("seq", "head"),
        P("seq", "head"),
        P("seq", "head"),
        P("seq", "head"),
        P("seq", "head"),
    )
    return jax.shard_map(shards, mesh=mesh, in_specs=in_specs, out_specs=out_specs, check_vma=False)
```

profile of v0, /device:TPU:196, one launch (start us, length us, event | category | flops | bytes accessed | tf_op | source)
XLA Modules:
  0.0 654.8 jit_solution(12983805571905351696)
XLA Ops:
  9.7 287.4 %while.32 = (s32[]{:T(128)}, bf16[25,2,128,128]{3,2,1,0:T(8,128)(2,1)}, bf16[2,128,128]{2,1,0:T(8,128)(2,1)S(1)}, s32[]{:T(128)}, s32[]{:T(128)}, /*index=5*/s32[]{:T(128)}) while((s32[]{:T(128)}, bf16[25,2,128,128]{3,2,1,0:T(8,128)(2,1)}, bf16[2,128,128]{2,1,0:T(8,128)(2,1)S(1)}, s32[]{:T(128)}, s32[]{:T(128)}, /*index=5*/s32[]{:T(128)}) %tuple.82), condition=%wide.region_1.2_spmd, body=%wide.region_0.0_spmd.sunk | while | flops 5 | bytes 524443 | solution.py:42
  9.7 5.5 collective-permute-start
  15.2 6.9 %collective-permute-done = bf16[2,128,128]{2,1,0:T(8,128)(2,1)S(1)} collective-permute-done((bf16[2,128,128]{2,1,0:T(8,128)(2,1)S(1)}, bf16[2,128,128]{2,1,0:T(8,128)(2,1)S(1)}, u32[]{:S(2)}, u32[]{:S(2)}) %collective-permute-start) | collective-permute-done | bytes 65568 | tf_op jit(solution)/shard_map/while/body/eval_jaxpr/ppermute | solution.py:16
  24.7 9.3 %collective-permute-done = bf16[2,128,128]{2,1,0:T(8,128)(2,1)S(1)} collective-permute-done((bf16[2,128,128]{2,1,0:T(8,128)(2,1)S(1)}, bf16[2,128,128]{2,1,0:T(8,128)(2,1)S(1)}, u32[]{:S(2)}, u32[]{:S(2)}) %collective-permute-start) | collective-permute-done | bytes 65568 | tf_op jit(solution)/shard_map/while/body/eval_jaxpr/ppermute | solution.py:16
  36.6 9.3 %collective-permute-done = bf16[2,128,128]{2,1,0:T(8,128)(2,1)S(1)} collective-permute-done((bf16[2,128,128]{2,1,0:T(8,128)(2,1)S(1)}, bf16[2,128,128]{2,1,0:T(8,128)(2,1)S(1)}, u32[]{:S(2)}, u32[]{:S(2)}) %collective-permute-start) | collective-permute-done | bytes 65568 | tf_op jit(solution)/shard_map/while/body/eval_jaxpr/ppermute | solution.py:16
  48.5 9.3 %collective-permute-done = bf16[2,128,128]{2,1,0:T(8,128)(2,1)S(1)} collective-permute-done((bf16[2,128,128]{2,1,0:T(8,128)(2,1)S(1)}, bf16[2,128,128]{2,1,0:T(8,128)(2,1)S(1)}, u32[]{:S(2)}, u32[]{:S(2)}) %collective-permute-start) | collective-permute-done | bytes 65568 | tf_op jit(solution)/shard_map/while/body/eval_jaxpr/ppermute | solution.py:16
  60.4 9.3 %collective-permute-done = bf16[2,128,128]{2,1,0:T(8,128)(2,1)S(1)} collective-permute-done((bf16[2,128,128]{2,1,0:T(8,128)(2,1)S(1)}, bf16[2,128,128]{2,1,0:T(8,128)(2,1)S(1)}, u32[]{:S(2)}, u32[]{:S(2)}) %collective-permute-start) | collective-permute-done | bytes 65568 | tf_op jit(solution)/shard_map/while/body/eval_jaxpr/ppermute | solution.py:16
  72.3 9.3 %collective-permute-done = bf16[2,128,128]{2,1,0:T(8,128)(2,1)S(1)} collective-permute-done((bf16[2,128,128]{2,1,0:T(8,128)(2,1)S(1)}, bf16[2,128,128]{2,1,0:T(8,128)(2,1)S(1)}, u32[]{:S(2)}, u32[]{:S(2)}) %collective-permute-start) | collective-permute-done | bytes 65568 | tf_op jit(solution)/shard_map/while/body/eval_jaxpr/ppermute | solution.py:16
  84.2 9.3 %collective-permute-done = bf16[2,128,128]{2,1,0:T(8,128)(2,1)S(1)} collective-permute-done((bf16[2,128,128]{2,1,0:T(8,128)(2,1)S(1)}, bf16[2,128,128]{2,1,0:T(8,128)(2,1)S(1)}, u32[]{:S(2)}, u32[]{:S(2)}) %collective-permute-start) | collective-permute-done | bytes 65568 | tf_op jit(solution)/shard_map/while/body/eval_jaxpr/ppermute | solution.py:16
  96.1 9.3 %collective-permute-done = bf16[2,128,128]{2,1,0:T(8,128)(2,1)S(1)} collective-permute-done((bf16[2,128,128]{2,1,0:T(8,128)(2,1)S(1)}, bf16[2,128,128]{2,1,0:T(8,128)(2,1)S(1)}, u32[]{:S(2)}, u32[]{:S(2)}) %collective-permute-start) | collective-permute-done | bytes 65568 | tf_op jit(solution)/shard_map/while/body/eval_jaxpr/ppermute | solution.py:16
  108.0 9.4 %collective-permute-done = bf16[2,128,128]{2,1,0:T(8,128)(2,1)S(1)} collective-permute-done((bf16[2,128,128]{2,1,0:T(8,128)(2,1)S(1)}, bf16[2,128,128]{2,1,0:T(8,128)(2,1)S(1)}, u32[]{:S(2)}, u32[]{:S(2)}) %collective-permute-start) | collective-permute-done | bytes 65568 | tf_op jit(solution)/shard_map/while/body/eval_jaxpr/ppermute | solution.py:16
  119.9 9.5 %collective-permute-done = bf16[2,128,128]{2,1,0:T(8,128)(2,1)S(1)} collective-permute-done((bf16[2,128,128]{2,1,0:T(8,128)(2,1)S(1)}, bf16[2,128,128]{2,1,0:T(8,128)(2,1)S(1)}, u32[]{:S(2)}, u32[]{:S(2)}) %collective-permute-start) | collective-permute-done | bytes 65568 | tf_op jit(solution)/shard_map/while/body/eval_jaxpr/ppermute | solution.py:16
  132.0 9.3 %collective-permute-done = bf16[2,128,128]{2,1,0:T(8,128)(2,1)S(1)} collective-permute-done((bf16[2,128,128]{2,1,0:T(8,128)(2,1)S(1)}, bf16[2,128,128]{2,1,0:T(8,128)(2,1)S(1)}, u32[]{:S(2)}, u32[]{:S(2)}) %collective-permute-start) | collective-permute-done | bytes 65568 | tf_op jit(solution)/shard_map/while/body/eval_jaxpr/ppermute | solution.py:16
  143.9 9.3 %collective-permute-done = bf16[2,128,128]{2,1,0:T(8,128)(2,1)S(1)} collective-permute-done((bf16[2,128,128]{2,1,0:T(8,128)(2,1)S(1)}, bf16[2,128,128]{2,1,0:T(8,128)(2,1)S(1)}, u32[]{:S(2)}, u32[]{:S(2)}) %collective-permute-start) | collective-permute-done | bytes 65568 | tf_op jit(solution)/shard_map/while/body/eval_jaxpr/ppermute | solution.py:16
  155.8 9.3 %collective-permute-done = bf16[2,128,128]{2,1,0:T(8,128)(2,1)S(1)} collective-permute-done((bf16[2,128,128]{2,1,0:T(8,128)(2,1)S(1)}, bf16[2,128,128]{2,1,0:T(8,128)(2,1)S(1)}, u32[]{:S(2)}, u32[]{:S(2)}) %collective-permute-start) | collective-permute-done | bytes 65568 | tf_op jit(solution)/shard_map/while/body/eval_jaxpr/ppermute | solution.py:16
  167.7 9.3 %collective-permute-done = bf16[2,128,128]{2,1,0:T(8,128)(2,1)S(1)} collective-permute-done((bf16[2,128,128]{2,1,0:T(8,128)(2,1)S(1)}, bf16[2,128,128]{2,1,0:T(8,128)(2,1)S(1)}, u32[]{:S(2)}, u32[]{:S(2)}) %collective-permute-start) | collective-permute-done | bytes 65568 | tf_op jit(solution)/shard_map/while/body/eval_jaxpr/ppermute | solution.py:16
  179.6 9.3 %collective-permute-done = bf16[2,128,128]{2,1,0:T(8,128)(2,1)S(1)} collective-permute-done((bf16[2,128,128]{2,1,0:T(8,128)(2,1)S(1)}, bf16[2,128,128]{2,1,0:T(8,128)(2,1)S(1)}, u32[]{:S(2)}, u32[]{:S(2)}) %collective-permute-start) | collective-permute-done | bytes 65568 | tf_op jit(solution)/shard_map/while/body/eval_jaxpr/ppermute | solution.py:16
  191.5 9.3 %collective-permute-done = bf16[2,128,128]{2,1,0:T(8,128)(2,1)S(1)} collective-permute-done((bf16[2,128,128]{2,1,0:T(8,128)(2,1)S(1)}, bf16[2,128,128]{2,1,0:T(8,128)(2,1)S(1)}, u32[]{:S(2)}, u32[]{:S(2)}) %collective-permute-start) | collective-permute-done | bytes 65568 | tf_op jit(solution)/shard_map/while/body/eval_jaxpr/ppermute | solution.py:16
  203.4 9.3 %collective-permute-done = bf16[2,128,128]{2,1,0:T(8,128)(2,1)S(1)} collective-permute-done((bf16[2,128,128]{2,1,0:T(8,128)(2,1)S(1)}, bf16[2,128,128]{2,1,0:T(8,128)(2,1)S(1)}, u32[]{:S(2)}, u32[]{:S(2)}) %collective-permute-start) | collective-permute-done | bytes 65568 | tf_op jit(solution)/shard_map/while/body/eval_jaxpr/ppermute | solution.py:16
  215.3 9.3 %collective-permute-done = bf16[2,128,128]{2,1,0:T(8,128)(2,1)S(1)} collective-permute-done((bf16[2,128,128]{2,1,0:T(8,128)(2,1)S(1)}, bf16[2,128,128]{2,1,0:T(8,128)(2,1)S(1)}, u32[]{:S(2)}, u32[]{:S(2)}) %collective-permute-start) | collective-permute-done | bytes 65568 | tf_op jit(solution)/shard_map/while/body/eval_jaxpr/ppermute | solution.py:16
  227.2 9.8 %collective-permute-done = bf16[2,128,128]{2,1,0:T(8,128)(2,1)S(1)} collective-permute-done((bf16[2,128,128]{2,1,0:T(8,128)(2,1)S(1)}, bf16[2,128,128]{2,1,0:T(8,128)(2,1)S(1)}, u32[]{:S(2)}, u32[]{:S(2)}) %collective-permute-start) | collective-permute-done | bytes 65568 | tf_op jit(solution)/shard_map/while/body/eval_jaxpr/ppermute | solution.py:16
  239.5 9.3 %collective-permute-done = bf16[2,128,128]{2,1,0:T(8,128)(2,1)S(1)} collective-permute-done((bf16[2,128,128]{2,1,0:T(8,128)(2,1)S(1)}, bf16[2,128,128]{2,1,0:T(8,128)(2,1)S(1)}, u32[]{:S(2)}, u32[]{:S(2)}) %collective-permute-start) | collective-permute-done | bytes 65568 | tf_op jit(solution)/shard_map/while/body/eval_jaxpr/ppermute | solution.py:16
  251.4 9.3 %collective-permute-done = bf16[2,128,128]{2,1,0:T(8,128)(2,1)S(1)} collective-permute-done((bf16[2,128,128]{2,1,0:T(8,128)(2,1)S(1)}, bf16[2,128,128]{2,1,0:T(8,128)(2,1)S(1)}, u32[]{:S(2)}, u32[]{:S(2)}) %collective-permute-start) | collective-permute-done | bytes 65568 | tf_op jit(solution)/shard_map/while/body/eval_jaxpr/ppermute | solution.py:16
  263.3 9.3 %collective-permute-done = bf16[2,128,128]{2,1,0:T(8,128)(2,1)S(1)} collective-permute-done((bf16[2,128,128]{2,1,0:T(8,128)(2,1)S(1)}, bf16[2,128,128]{2,1,0:T(8,128)(2,1)S(1)}, u32[]{:S(2)}, u32[]{:S(2)}) %collective-permute-start) | collective-permute-done | bytes 65568 | tf_op jit(solution)/shard_map/while/body/eval_jaxpr/ppermute | solution.py:16
  275.2 9.3 %collective-permute-done = bf16[2,128,128]{2,1,0:T(8,128)(2,1)S(1)} collective-permute-done((bf16[2,128,128]{2,1,0:T(8,128)(2,1)S(1)}, bf16[2,128,128]{2,1,0:T(8,128)(2,1)S(1)}, u32[]{:S(2)}, u32[]{:S(2)}) %collective-permute-start) | collective-permute-done | bytes 65568 | tf_op jit(solution)/shard_map/while/body/eval_jaxpr/ppermute | solution.py:16
  287.1 9.4 %collective-permute-done = bf16[2,128,128]{2,1,0:T(8,128)(2,1)S(1)} collective-permute-done((bf16[2,128,128]{2,1,0:T(8,128)(2,1)S(1)}, bf16[2,128,128]{2,1,0:T(8,128)(2,1)S(1)}, u32[]{:S(2)}, u32[]{:S(2)}) %collective-permute-start) | collective-permute-done | bytes 65568 | tf_op jit(solution)/shard_map/while/body/eval_jaxpr/ppermute | solution.py:16
  297.2 2.9 copy.58
  301.0 21.5 %all_gather.3 = bf16[128,3072]{1,0:T(8,128)(2,1)S(1)} all-gather(bf16[128,384]{1,0:T(8,128)(2,1)S(1)} %copy-done.6), channel_id=1, replica_groups=mesh['seq'=96,'head'=8] {'head'}, dimensions={1}, use_global_device_ids=true | all-gather | bytes 884736 | tf_op jit(solution)/shard_map/all_gather | solution.py:73
  326.0 2.1 compare_and_fusion
  328.1 2.2 fusion.17
  335.1 2.3 copy.84
  338.3 4.7 convolution_bitcast_fusion.1
  344.8 2.0 fusion.7
  347.5 2.7 copy.70
  350.2 4.1 pad_maximum_fusion
  354.2 290.6 %while.33 = (s32[]{:T(128)}, f32[2,128,128]{2,1,0:T(8,128)S(1)}, f32[25,2,128,128]{3,2,0,1:T(8,128)}, s32[]{:T(128)}, s32[]{:T(128)}, /*index=5*/s32[]{:T(128)}, s32[]{:T(128)}) while((s32[]{:T(128)}, f32[2,128,128]{2,1,0:T(8,128)S(1)}, f32[25,2,128,128]{3,2,0,1:T(8,128)}, s32[]{:T(128)}, s32[]{:T(128)}, /*index=5*/s32[]{:T(128)}, ...), condition=%wide.region_10.11_spmd.clone, body=%wide.region_9.10_spmd.clone.sunk | while | flops 131079 | bytes 786609 | solution.py:112
  355.1 1.9 collective-permute-start.1
  357.1 6.6 %collective-permute-done.1 = bf16[2,128,128]{2,1,0:T(8,128)(2,1)S(1)} collective-permute-done((bf16[2,128,128]{2,1,0:T(8,128)(2,1)S(1)}, bf16[2,128,128]{2,1,0:T(8,128)(2,1)S(1)}, u32[]{:S(2)}, u32[]{:S(2)}) %collective-permute-start.1) | collective-permute-done | bytes 65568 | tf_op jit(solution)/shard_map/while/body/eval_jaxpr/ppermute | solution.py:16
  364.6 6.5 collective-permute-start.1
  371.1 3.0 collective-permute-done.1
  375.1 9.6 %collective-permute-start.1 = (bf16[2,128,128]{2,1,0:T(8,128)(2,1)S(1)}, bf16[2,128,128]{2,1,0:T(8,128)(2,1)S(1)}, u32[]{:S(2)}, u32[]{:S(2)}) collective-permute-start(bf16[2,128,128]{2,1,0:T(8,128)(2,1)S(1)} %fusion.33), channel_id=1, source_target_pairs={{8,0},{16,8},{24,16},{32,24},{40,32},{48,40},{56,48},{64,56},{72,6... | collective-permute-start | bytes 196616 | tf_op jit(solution)/shard_map/while/body/eval_jaxpr/ppermute | solution.py:16
  387.5 9.4 %collective-permute-start.1 = (bf16[2,128,128]{2,1,0:T(8,128)(2,1)S(1)}, bf16[2,128,128]{2,1,0:T(8,128)(2,1)S(1)}, u32[]{:S(2)}, u32[]{:S(2)}) collective-permute-start(bf16[2,128,128]{2,1,0:T(8,128)(2,1)S(1)} %fusion.33), channel_id=1, source_target_pairs={{8,0},{16,8},{24,16},{32,24},{40,32},{48,40},{56,48},{64,56},{72,6... | collective-permute-start | bytes 196616 | tf_op jit(solution)/shard_map/while/body/eval_jaxpr/ppermute | solution.py:16
  399.8 9.4 %collective-permute-start.1 = (bf16[2,128,128]{2,1,0:T(8,128)(2,1)S(1)}, bf16[2,128,128]{2,1,0:T(8,128)(2,1)S(1)}, u32[]{:S(2)}, u32[]{:S(2)}) collective-permute-start(bf16[2,128,128]{2,1,0:T(8,128)(2,1)S(1)} %fusion.33), channel_id=1, source_target_pairs={{8,0},{16,8},{24,16},{32,24},{40,32},{48,40},{56,48},{64,56},{72,6... | collective-permute-start | bytes 196616 | tf_op jit(solution)/shard_map/while/body/eval_jaxpr/ppermute | solution.py:16
  412.0 9.4 %collective-permute-start.1 = (bf16[2,128,128]{2,1,0:T(8,128)(2,1)S(1)}, bf16[2,128,128]{2,1,0:T(8,128)(2,1)S(1)}, u32[]{:S(2)}, u32[]{:S(2)}) collective-permute-start(bf16[2,128,128]{2,1,0:T(8,128)(2,1)S(1)} %fusion.33), channel_id=1, source_target_pairs={{8,0},{16,8},{24,16},{32,24},{40,32},{48,40},{56,48},{64,56},{72,6... | collective-permute-start | bytes 196616 | tf_op jit(solution)/shard_map/while/body/eval_jaxpr/ppermute | solution.py:16
  424.3 9.4 %collective-permute-start.1 = (bf16[2,128,128]{2,1,0:T(8,128)(2,1)S(1)}, bf16[2,128,128]{2,1,0:T(8,128)(2,1)S(1)}, u32[]{:S(2)}, u32[]{:S(2)}) collective-permute-start(bf16[2,128,128]{2,1,0:T(8,128)(2,1)S(1)} %fusion.33), channel_id=1, source_target_pairs={{8,0},{16,8},{24,16},{32,24},{40,32},{48,40},{56,48},{64,56},{72,6... | collective-permute-start | bytes 196616 | tf_op jit(solution)/shard_map/while/body/eval_jaxpr/ppermute | solution.py:16
  436.5 9.4 %collective-permute-start.1 = (bf16[2,128,128]{2,1,0:T(8,128)(2,1)S(1)}, bf16[2,128,128]{2,1,0:T(8,128)(2,1)S(1)}, u32[]{:S(2)}, u32[]{:S(2)}) collective-permute-start(bf16[2,128,128]{2,1,0:T(8,128)(2,1)S(1)} %fusion.33), channel_id=1, source_target_pairs={{8,0},{16,8},{24,16},{32,24},{40,32},{48,40},{56,48},{64,56},{72,6... | collective-permute-start | bytes 196616 | tf_op jit(solution)/shard_map/while/body/eval_jaxpr/ppermute | solution.py:16
  448.8 9.4 %collective-permute-start.1 = (bf16[2,128,128]{2,1,0:T(8,128)(2,1)S(1)}, bf16[2,128,128]{2,1,0:T(8,128)(2,1)S(1)}, u32[]{:S(2)}, u32[]{:S(2)}) collective-permute-start(bf16[2,128,128]{2,1,0:T(8,128)(2,1)S(1)} %fusion.33), channel_id=1, source_target_pairs={{8,0},{16,8},{24,16},{32,24},{40,32},{48,40},{56,48},{64,56},{72,6... | collective-permute-start | bytes 196616 | tf_op jit(solution)/shard_map/while/body/eval_jaxpr/ppermute | solution.py:16
  461.0 9.4 %collective-permute-start.1 = (bf16[2,128,128]{2,1,0:T(8,128)(2,1)S(1)}, bf16[2,128,128]{2,1,0:T(8,128)(2,1)S(1)}, u32[]{:S(2)}, u32[]{:S(2)}) collective-permute-start(bf16[2,128,128]{2,1,0:T(8,128)(2,1)S(1)} %fusion.33), channel_id=1, source_target_pairs={{8,0},{16,8},{24,16},{32,24},{40,32},{48,40},{56,48},{64,56},{72,6... | collective-permute-start | bytes 196616 | tf_op jit(solution)/shard_map/while/body/eval_jaxpr/ppermute | solution.py:16
  473.2 9.4 %collective-permute-start.1 = (bf16[2,128,128]{2,1,0:T(8,128)(2,1)S(1)}, bf16[2,128,128]{2,1,0:T(8,128)(2,1)S(1)}, u32[]{:S(2)}, u32[]{:S(2)}) collective-permute-start(bf16[2,128,128]{2,1,0:T(8,128)(2,1)S(1)} %fusion.33), channel_id=1, source_target_pairs={{8,0},{16,8},{24,16},{32,24},{40,32},{48,40},{56,48},{64,56},{72,6... | collective-permute-start | bytes 196616 | tf_op jit(solution)/shard_map/while/body/eval_jaxpr/ppermute | solution.py:16
  482.6 2.1 collective-permute-done.1
  485.7 9.5 %collective-permute-start.1 = (bf16[2,128,128]{2,1,0:T(8,128)(2,1)S(1)}, bf16[2,128,128]{2,1,0:T(8,128)(2,1)S(1)}, u32[]{:S(2)}, u32[]{:S(2)}) collective-permute-start(bf16[2,128,128]{2,1,0:T(8,128)(2,1)S(1)} %fusion.33), channel_id=1, source_target_pairs={{8,0},{16,8},{24,16},{32,24},{40,32},{48,40},{56,48},{64,56},{72,6... | collective-permute-start | bytes 196616 | tf_op jit(solution)/shard_map/while/body/eval_jaxpr/ppermute | solution.py:16
  498.1 9.4 %collective-permute-start.1 = (bf16[2,128,128]{2,1,0:T(8,128)(2,1)S(1)}, bf16[2,128,128]{2,1,0:T(8,128)(2,1)S(1)}, u32[]{:S(2)}, u32[]{:S(2)}) collective-permute-start(bf16[2,128,128]{2,1,0:T(8,128)(2,1)S(1)} %fusion.33), channel_id=1, source_target_pairs={{8,0},{16,8},{24,16},{32,24},{40,32},{48,40},{56,48},{64,56},{72,6... | collective-permute-start | bytes 196616 | tf_op jit(solution)/shard_map/while/body/eval_jaxpr/ppermute | solution.py:16
  510.4 9.4 %collective-permute-start.1 = (bf16[2,128,128]{2,1,0:T(8,128)(2,1)S(1)}, bf16[2,128,128]{2,1,0:T(8,128)(2,1)S(1)}, u32[]{:S(2)}, u32[]{:S(2)}) collective-permute-start(bf16[2,128,128]{2,1,0:T(8,128)(2,1)S(1)} %fusion.33), channel_id=1, source_target_pairs={{8,0},{16,8},{24,16},{32,24},{40,32},{48,40},{56,48},{64,56},{72,6... | collective-permute-start | bytes 196616 | tf_op jit(solution)/shard_map/while/body/eval_jaxpr/ppermute | solution.py:16
  522.6 9.4 %collective-permute-start.1 = (bf16[2,128,128]{2,1,0:T(8,128)(2,1)S(1)}, bf16[2,128,128]{2,1,0:T(8,128)(2,1)S(1)}, u32[]{:S(2)}, u32[]{:S(2)}) collective-permute-start(bf16[2,128,128]{2,1,0:T(8,128)(2,1)S(1)} %fusion.33), channel_id=1, source_target_pairs={{8,0},{16,8},{24,16},{32,24},{40,32},{48,40},{56,48},{64,56},{72,6... | collective-permute-start | bytes 196616 | tf_op jit(solution)/shard_map/while/body/eval_jaxpr/ppermute | solution.py:16
  534.9 9.4 %collective-permute-start.1 = (bf16[2,128,128]{2,1,0:T(8,128)(2,1)S(1)}, bf16[2,128,128]{2,1,0:T(8,128)(2,1)S(1)}, u32[]{:S(2)}, u32[]{:S(2)}) collective-permute-start(bf16[2,128,128]{2,1,0:T(8,128)(2,1)S(1)} %fusion.33), channel_id=1, source_target_pairs={{8,0},{16,8},{24,16},{32,24},{40,32},{48,40},{56,48},{64,56},{72,6... | collective-permute-start | bytes 196616 | tf_op jit(solution)/shard_map/while/body/eval_jaxpr/ppermute | solution.py:16
  547.1 9.4 %collective-permute-start.1 = (bf16[2,128,128]{2,1,0:T(8,128)(2,1)S(1)}, bf16[2,128,128]{2,1,0:T(8,128)(2,1)S(1)}, u32[]{:S(2)}, u32[]{:S(2)}) collective-permute-start(bf16[2,128,128]{2,1,0:T(8,128)(2,1)S(1)} %fusion.33), channel_id=1, source_target_pairs={{8,0},{16,8},{24,16},{32,24},{40,32},{48,40},{56,48},{64,56},{72,6... | collective-permute-start | bytes 196616 | tf_op jit(solution)/shard_map/while/body/eval_jaxpr/ppermute | solution.py:16
  559.4 9.4 %collective-permute-start.1 = (bf16[2,128,128]{2,1,0:T(8,128)(2,1)S(1)}, bf16[2,128,128]{2,1,0:T(8,128)(2,1)S(1)}, u32[]{:S(2)}, u32[]{:S(2)}) collective-permute-start(bf16[2,128,128]{2,1,0:T(8,128)(2,1)S(1)} %fusion.33), channel_id=1, source_target_pairs={{8,0},{16,8},{24,16},{32,24},{40,32},{48,40},{56,48},{64,56},{72,6... | collective-permute-start | bytes 196616 | tf_op jit(solution)/shard_map/while/body/eval_jaxpr/ppermute | solution.py:16
  571.6 9.4 %collective-permute-start.1 = (bf16[2,128,128]{2,1,0:T(8,128)(2,1)S(1)}, bf16[2,128,128]{2,1,0:T(8,128)(2,1)S(1)}, u32[]{:S(2)}, u32[]{:S(2)}) collective-permute-start(bf16[2,128,128]{2,1,0:T(8,128)(2,1)S(1)} %fusion.33), channel_id=1, source_target_pairs={{8,0},{16,8},{24,16},{32,24},{40,32},{48,40},{56,48},{64,56},{72,6... | collective-permute-start | bytes 196616 | tf_op jit(solution)/shard_map/while/body/eval_jaxpr/ppermute | solution.py:16
  583.8 9.4 %collective-permute-start.1 = (bf16[2,128,128]{2,1,0:T(8,128)(2,1)S(1)}, bf16[2,128,128]{2,1,0:T(8,128)(2,1)S(1)}, u32[]{:S(2)}, u32[]{:S(2)}) collective-permute-start(bf16[2,128,128]{2,1,0:T(8,128)(2,1)S(1)} %fusion.33), channel_id=1, source_target_pairs={{8,0},{16,8},{24,16},{32,24},{40,32},{48,40},{56,48},{64,56},{72,6... | collective-permute-start | bytes 196616 | tf_op jit(solution)/shard_map/while/body/eval_jaxpr/ppermute | solution.py:16
  596.1 9.4 %collective-permute-start.1 = (bf16[2,128,128]{2,1,0:T(8,128)(2,1)S(1)}, bf16[2,128,128]{2,1,0:T(8,128)(2,1)S(1)}, u32[]{:S(2)}, u32[]{:S(2)}) collective-permute-start(bf16[2,128,128]{2,1,0:T(8,128)(2,1)S(1)} %fusion.33), channel_id=1, source_target_pairs={{8,0},{16,8},{24,16},{32,24},{40,32},{48,40},{56,48},{64,56},{72,6... | collective-permute-start | bytes 196616 | tf_op jit(solution)/shard_map/while/body/eval_jaxpr/ppermute | solution.py:16
  605.5 2.4 collective-permute-done.1
  608.9 9.5 %collective-permute-start.1 = (bf16[2,128,128]{2,1,0:T(8,128)(2,1)S(1)}, bf16[2,128,128]{2,1,0:T(8,128)(2,1)S(1)}, u32[]{:S(2)}, u32[]{:S(2)}) collective-permute-start(bf16[2,128,128]{2,1,0:T(8,128)(2,1)S(1)} %fusion.33), channel_id=1, source_target_pairs={{8,0},{16,8},{24,16},{32,24},{40,32},{48,40},{56,48},{64,56},{72,6... | collective-permute-start | bytes 196616 | tf_op jit(solution)/shard_map/while/body/eval_jaxpr/ppermute | solution.py:16
  621.2 9.4 %collective-permute-start.1 = (bf16[2,128,128]{2,1,0:T(8,128)(2,1)S(1)}, bf16[2,128,128]{2,1,0:T(8,128)(2,1)S(1)}, u32[]{:S(2)}, u32[]{:S(2)}) collective-permute-start(bf16[2,128,128]{2,1,0:T(8,128)(2,1)S(1)} %fusion.33), channel_id=1, source_target_pairs={{8,0},{16,8},{24,16},{32,24},{40,32},{48,40},{56,48},{64,56},{72,6... | collective-permute-start | bytes 196616 | tf_op jit(solution)/shard_map/while/body/eval_jaxpr/ppermute | solution.py:16
  633.5 9.4 %collective-permute-start.1 = (bf16[2,128,128]{2,1,0:T(8,128)(2,1)S(1)}, bf16[2,128,128]{2,1,0:T(8,128)(2,1)S(1)}, u32[]{:S(2)}, u32[]{:S(2)}) collective-permute-start(bf16[2,128,128]{2,1,0:T(8,128)(2,1)S(1)} %fusion.33), channel_id=1, source_target_pairs={{8,0},{16,8},{24,16},{32,24},{40,32},{48,40},{56,48},{64,56},{72,6... | collective-permute-start | bytes 196616 | tf_op jit(solution)/shard_map/while/body/eval_jaxpr/ppermute | solution.py:16
  (186 shorter events, 137.6 us)
Async XLA Ops:
  7.2 315.4 %copy-start = (bf16[384,3072]{1,0:T(8,128)(2,1)S(1)}, bf16[384,3072]{1,0:T(8,128)(2,1)}, u32[]{:S(2)}) copy-start(bf16[384,3072]{1,0:T(8,128)(2,1)} %param.15) | copy-start | bytes 7077892
  7.2 639.1 %reduce-scatter.4.cloned.1.call-start = ((), (), s32[]{:S(2)}) async-start(), calls=%async_computation.1 | async-start | bytes 884736
  9.7 12.4 %collective-permute-start = (bf16[2,128,128]{2,1,0:T(8,128)(2,1)S(1)}, bf16[2,128,128]{2,1,0:T(8,128)(2,1)S(1)}, u32[]{:S(2)}, u32[]{:S(2)}) collective-permute-start(bf16[2,128,128]{2,1,0:T(8,128)(2,1)S(1)} %get-tuple-element.278), channel_id=1, source_target_pairs={{0,8},{8,16},{16,24},{24,32},{32,40},{40,48},{48,56},{56,64},{64,7... | collective-permute-start | bytes 196616 | tf_op jit(solution)/shard_map/while/body/eval_jaxpr/ppermute | solution.py:16
  22.8 11.3 %collective-permute-start = (bf16[2,128,128]{2,1,0:T(8,128)(2,1)S(1)}, bf16[2,128,128]{2,1,0:T(8,128)(2,1)S(1)}, u32[]{:S(2)}, u32[]{:S(2)}) collective-permute-start(bf16[2,128,128]{2,1,0:T(8,128)(2,1)S(1)} %get-tuple-element.278), channel_id=1, source_target_pairs={{0,8},{8,16},{16,24},{24,32},{32,40},{40,48},{48,56},{56,64},{64,7... | collective-permute-start | bytes 196616 | tf_op jit(solution)/shard_map/while/body/eval_jaxpr/ppermute | solution.py:16
  34.7 11.3 %collective-permute-start = (bf16[2,128,128]{2,1,0:T(8,128)(2,1)S(1)}, bf16[2,128,128]{2,1,0:T(8,128)(2,1)S(1)}, u32[]{:S(2)}, u32[]{:S(2)}) collective-permute-start(bf16[2,128,128]{2,1,0:T(8,128)(2,1)S(1)} %get-tuple-element.278), channel_id=1, source_target_pairs={{0,8},{8,16},{16,24},{24,32},{32,40},{40,48},{48,56},{56,64},{64,7... | collective-permute-start | bytes 196616 | tf_op jit(solution)/shard_map/while/body/eval_jaxpr/ppermute | solution.py:16
  46.6 11.3 %collective-permute-start = (bf16[2,128,128]{2,1,0:T(8,128)(2,1)S(1)}, bf16[2,128,128]{2,1,0:T(8,128)(2,1)S(1)}, u32[]{:S(2)}, u32[]{:S(2)}) collective-permute-start(bf16[2,128,128]{2,1,0:T(8,128)(2,1)S(1)} %get-tuple-element.278), channel_id=1, source_target_pairs={{0,8},{8,16},{16,24},{24,32},{32,40},{40,48},{48,56},{56,64},{64,7... | collective-permute-start | bytes 196616 | tf_op jit(solution)/shard_map/while/body/eval_jaxpr/ppermute | solution.py:16
  58.5 11.3 %collective-permute-start = (bf16[2,128,128]{2,1,0:T(8,128)(2,1)S(1)}, bf16[2,128,128]{2,1,0:T(8,128)(2,1)S(1)}, u32[]{:S(2)}, u32[]{:S(2)}) collective-permute-start(bf16[2,128,128]{2,1,0:T(8,128)(2,1)S(1)} %get-tuple-element.278), channel_id=1, source_target_pairs={{0,8},{8,16},{16,24},{24,32},{32,40},{40,48},{48,56},{56,64},{64,7... | collective-permute-start | bytes 196616 | tf_op jit(solution)/shard_map/while/body/eval_jaxpr/ppermute | solution.py:16
  70.4 11.3 %collective-permute-start = (bf16[2,128,128]{2,1,0:T(8,128)(2,1)S(1)}, bf16[2,128,128]{2,1,0:T(8,128)(2,1)S(1)}, u32[]{:S(2)}, u32[]{:S(2)}) collective-permute-start(bf16[2,128,128]{2,1,0:T(8,128)(2,1)S(1)} %get-tuple-element.278), channel_id=1, source_target_pairs={{0,8},{8,16},{16,24},{24,32},{32,40},{40,48},{48,56},{56,64},{64,7... | collective-permute-start | bytes 196616 | tf_op jit(solution)/shard_map/while/body/eval_jaxpr/ppermute | solution.py:16
  82.3 11.3 %collective-permute-start = (bf16[2,128,128]{2,1,0:T(8,128)(2,1)S(1)}, bf16[2,128,128]{2,1,0:T(8,128)(2,1)S(1)}, u32[]{:S(2)}, u32[]{:S(2)}) collective-permute-start(bf16[2,128,128]{2,1,0:T(8,128)(2,1)S(1)} %get-tuple-element.278), channel_id=1, source_target_pairs={{0,8},{8,16},{16,24},{24,32},{32,40},{40,48},{48,56},{56,64},{64,7... | collective-permute-start | bytes 196616 | tf_op jit(solution)/shard_map/while/body/eval_jaxpr/ppermute | solution.py:16
  94.1 11.3 %collective-permute-start = (bf16[2,128,128]{2,1,0:T(8,128)(2,1)S(1)}, bf16[2,128,128]{2,1,0:T(8,128)(2,1)S(1)}, u32[]{:S(2)}, u32[]{:S(2)}) collective-permute-start(bf16[2,128,128]{2,1,0:T(8,128)(2,1)S(1)} %get-tuple-element.278), channel_id=1, source_target_pairs={{0,8},{8,16},{16,24},{24,32},{32,40},{40,48},{48,56},{56,64},{64,7... | collective-permute-start | bytes 196616 | tf_op jit(solution)/shard_map/while/body/eval_jaxpr/ppermute | solution.py:16
  106.0 11.3 %collective-permute-start = (bf16[2,128,128]{2,1,0:T(8,128)(2,1)S(1)}, bf16[2,128,128]{2,1,0:T(8,128)(2,1)S(1)}, u32[]{:S(2)}, u32[]{:S(2)}) collective-permute-start(bf16[2,128,128]{2,1,0:T(8,128)(2,1)S(1)} %get-tuple-element.278), channel_id=1, source_target_pairs={{0,8},{8,16},{16,24},{24,32},{32,40},{40,48},{48,56},{56,64},{64,7... | collective-permute-start | bytes 196616 | tf_op jit(solution)/shard_map/while/body/eval_jaxpr/ppermute | solution.py:16
  118.0 11.5 %collective-permute-start = (bf16[2,128,128]{2,1,0:T(8,128)(2,1)S(1)}, bf16[2,128,128]{2,1,0:T(8,128)(2,1)S(1)}, u32[]{:S(2)}, u32[]{:S(2)}) collective-permute-start(bf16[2,128,128]{2,1,0:T(8,128)(2,1)S(1)} %get-tuple-element.278), channel_id=1, source_target_pairs={{0,8},{8,16},{16,24},{24,32},{32,40},{40,48},{48,56},{56,64},{64,7... | collective-permute-start | bytes 196616 | tf_op jit(solution)/shard_map/while/body/eval_jaxpr/ppermute | solution.py:16
  130.1 11.3 %collective-permute-start = (bf16[2,128,128]{2,1,0:T(8,128)(2,1)S(1)}, bf16[2,128,128]{2,1,0:T(8,128)(2,1)S(1)}, u32[]{:S(2)}, u32[]{:S(2)}) collective-permute-start(bf16[2,128,128]{2,1,0:T(8,128)(2,1)S(1)} %get-tuple-element.278), channel_id=1, source_target_pairs={{0,8},{8,16},{16,24},{24,32},{32,40},{40,48},{48,56},{56,64},{64,7... | collective-permute-start | bytes 196616 | tf_op jit(solution)/shard_map/while/body/eval_jaxpr/ppermute | solution.py:16
  142.0 11.3 %collective-permute-start = (bf16[2,128,128]{2,1,0:T(8,128)(2,1)S(1)}, bf16[2,128,128]{2,1,0:T(8,128)(2,1)S(1)}, u32[]{:S(2)}, u32[]{:S(2)}) collective-permute-start(bf16[2,128,128]{2,1,0:T(8,128)(2,1)S(1)} %get-tuple-element.278), channel_id=1, source_target_pairs={{0,8},{8,16},{16,24},{24,32},{32,40},{40,48},{48,56},{56,64},{64,7... | collective-permute-start | bytes 196616 | tf_op jit(solution)/shard_map/while/body/eval_jaxpr/ppermute | solution.py:16
  153.9 11.3 %collective-permute-start = (bf16[2,128,128]{2,1,0:T(8,128)(2,1)S(1)}, bf16[2,128,128]{2,1,0:T(8,128)(2,1)S(1)}, u32[]{:S(2)}, u32[]{:S(2)}) collective-permute-start(bf16[2,128,128]{2,1,0:T(8,128)(2,1)S(1)} %get-tuple-element.278), channel_id=1, source_target_pairs={{0,8},{8,16},{16,24},{24,32},{32,40},{40,48},{48,56},{56,64},{64,7... | collective-permute-start | bytes 196616 | tf_op jit(solution)/shard_map/while/body/eval_jaxpr/ppermute | solution.py:16
  165.8 11.3 %collective-permute-start = (bf16[2,128,128]{2,1,0:T(8,128)(2,1)S(1)}, bf16[2,128,128]{2,1,0:T(8,128)(2,1)S(1)}, u32[]{:S(2)}, u32[]{:S(2)}) collective-permute-start(bf16[2,128,128]{2,1,0:T(8,128)(2,1)S(1)} %get-tuple-element.278), channel_id=1, source_target_pairs={{0,8},{8,16},{16,24},{24,32},{32,40},{40,48},{48,56},{56,64},{64,7... | collective-permute-start | bytes 196616 | tf_op jit(solution)/shard_map/while/body/eval_jaxpr/ppermute | solution.py:16
  177.7 11.3 %collective-permute-start = (bf16[2,128,128]{2,1,0:T(8,128)(2,1)S(1)}, bf16[2,128,128]{2,1,0:T(8,128)(2,1)S(1)}, u32[]{:S(2)}, u32[]{:S(2)}) collective-permute-start(bf16[2,128,128]{2,1,0:T(8,128)(2,1)S(1)} %get-tuple-element.278), channel_id=1, source_target_pairs={{0,8},{8,16},{16,24},{24,32},{32,40},{40,48},{48,56},{56,64},{64,7... | collective-permute-start | bytes 196616 | tf_op jit(solution)/shard_map/while/body/eval_jaxpr/ppermute | solution.py:16
  189.6 11.3 %collective-permute-start = (bf16[2,128,128]{2,1,0:T(8,128)(2,1)S(1)}, bf16[2,128,128]{2,1,0:T(8,128)(2,1)S(1)}, u32[]{:S(2)}, u32[]{:S(2)}) collective-permute-start(bf16[2,128,128]{2,1,0:T(8,128)(2,1)S(1)} %get-tuple-element.278), channel_id=1, source_target_pairs={{0,8},{8,16},{16,24},{24,32},{32,40},{40,48},{48,56},{56,64},{64,7... | collective-permute-start | bytes 196616 | tf_op jit(solution)/shard_map/while/body/eval_jaxpr/ppermute | solution.py:16
  201.5 11.3 %collective-permute-start = (bf16[2,128,128]{2,1,0:T(8,128)(2,1)S(1)}, bf16[2,128,128]{2,1,0:T(8,128)(2,1)S(1)}, u32[]{:S(2)}, u32[]{:S(2)}) collective-permute-start(bf16[2,128,128]{2,1,0:T(8,128)(2,1)S(1)} %get-tuple-element.278), channel_id=1, source_target_pairs={{0,8},{8,16},{16,24},{24,32},{32,40},{40,48},{48,56},{56,64},{64,7... | collective-permute-start | bytes 196616 | tf_op jit(solution)/shard_map/while/body/eval_jaxpr/ppermute | solution.py:16
  213.4 11.3 %collective-permute-start = (bf16[2,128,128]{2,1,0:T(8,128)(2,1)S(1)}, bf16[2,128,128]{2,1,0:T(8,128)(2,1)S(1)}, u32[]{:S(2)}, u32[]{:S(2)}) collective-permute-start(bf16[2,128,128]{2,1,0:T(8,128)(2,1)S(1)} %get-tuple-element.278), channel_id=1, source_target_pairs={{0,8},{8,16},{16,24},{24,32},{32,40},{40,48},{48,56},{56,64},{64,7... | collective-permute-start | bytes 196616 | tf_op jit(solution)/shard_map/while/body/eval_jaxpr/ppermute | solution.py:16
  225.3 11.7 %collective-permute-start = (bf16[2,128,128]{2,1,0:T(8,128)(2,1)S(1)}, bf16[2,128,128]{2,1,0:T(8,128)(2,1)S(1)}, u32[]{:S(2)}, u32[]{:S(2)}) collective-permute-start(bf16[2,128,128]{2,1,0:T(8,128)(2,1)S(1)} %get-tuple-element.278), channel_id=1, source_target_pairs={{0,8},{8,16},{16,24},{24,32},{32,40},{40,48},{48,56},{56,64},{64,7... | collective-permute-start | bytes 196616 | tf_op jit(solution)/shard_map/while/body/eval_jaxpr/ppermute | solution.py:16
  237.6 11.3 %collective-permute-start = (bf16[2,128,128]{2,1,0:T(8,128)(2,1)S(1)}, bf16[2,128,128]{2,1,0:T(8,128)(2,1)S(1)}, u32[]{:S(2)}, u32[]{:S(2)}) collective-permute-start(bf16[2,128,128]{2,1,0:T(8,128)(2,1)S(1)} %get-tuple-element.278), channel_id=1, source_target_pairs={{0,8},{8,16},{16,24},{24,32},{32,40},{40,48},{48,56},{56,64},{64,7... | collective-permute-start | bytes 196616 | tf_op jit(solution)/shard_map/while/body/eval_jaxpr/ppermute | solution.py:16
  249.5 11.3 %collective-permute-start = (bf16[2,128,128]{2,1,0:T(8,128)(2,1)S(1)}, bf16[2,128,128]{2,1,0:T(8,128)(2,1)S(1)}, u32[]{:S(2)}, u32[]{:S(2)}) collective-permute-start(bf16[2,128,128]{2,1,0:T(8,128)(2,1)S(1)} %get-tuple-element.278), channel_id=1, source_target_pairs={{0,8},{8,16},{16,24},{24,32},{32,40},{40,48},{48,56},{56,64},{64,7... | collective-permute-start | bytes 196616 | tf_op jit(solution)/shard_map/while/body/eval_jaxpr/ppermute | solution.py:16
  261.4 11.3 %collective-permute-start = (bf16[2,128,128]{2,1,0:T(8,128)(2,1)S(1)}, bf16[2,128,128]{2,1,0:T(8,128)(2,1)S(1)}, u32[]{:S(2)}, u32[]{:S(2)}) collective-permute-start(bf16[2,128,128]{2,1,0:T(8,128)(2,1)S(1)} %get-tuple-element.278), channel_id=1, source_target_pairs={{0,8},{8,16},{16,24},{24,32},{32,40},{40,48},{48,56},{56,64},{64,7... | collective-permute-start | bytes 196616 | tf_op jit(solution)/shard_map/while/body/eval_jaxpr/ppermute | solution.py:16
  273.3 11.3 %collective-permute-start = (bf16[2,128,128]{2,1,0:T(8,128)(2,1)S(1)}, bf16[2,128,128]{2,1,0:T(8,128)(2,1)S(1)}, u32[]{:S(2)}, u32[]{:S(2)}) collective-permute-start(bf16[2,128,128]{2,1,0:T(8,128)(2,1)S(1)} %get-tuple-element.278), channel_id=1, source_target_pairs={{0,8},{8,16},{16,24},{24,32},{32,40},{40,48},{48,56},{56,64},{64,7... | collective-permute-start | bytes 196616 | tf_op jit(solution)/shard_map/while/body/eval_jaxpr/ppermute | solution.py:16
  285.2 11.4 %collective-permute-start = (bf16[2,128,128]{2,1,0:T(8,128)(2,1)S(1)}, bf16[2,128,128]{2,1,0:T(8,128)(2,1)S(1)}, u32[]{:S(2)}, u32[]{:S(2)}) collective-permute-start(bf16[2,128,128]{2,1,0:T(8,128)(2,1)S(1)} %get-tuple-element.278), channel_id=1, source_target_pairs={{0,8},{8,16},{16,24},{24,32},{32,40},{40,48},{48,56},{56,64},{64,7... | collective-permute-start | bytes 196616 | tf_op jit(solution)/shard_map/while/body/eval_jaxpr/ppermute | solution.py:16
  297.2 2.9 copy-start.3
  297.2 3.9 copy-start.6
  322.5 2.8 copy-start.7
  322.5 3.0 copy-start.8
  330.2 2.3 copy-start.1
  330.2 2.3 copy-start.5
  338.3 4.7 copy-start.2
  343.0 1.2 copy-start.4
  355.1 8.5 %collective-permute-start.1 = (bf16[2,128,128]{2,1,0:T(8,128)(2,1)S(1)}, bf16[2,128,128]{2,1,0:T(8,128)(2,1)S(1)}, u32[]{:S(2)}, u32[]{:S(2)}) collective-permute-start(bf16[2,128,128]{2,1,0:T(8,128)(2,1)S(1)} %fusion.33), channel_id=1, source_target_pairs={{8,0},{16,8},{24,16},{32,24},{40,32},{48,40},{56,48},{64,56},{72,6... | collective-permute-start | bytes 196616 | tf_op jit(solution)/shard_map/while/body/eval_jaxpr/ppermute | solution.py:16
  364.6 9.5 %collective-permute-start.1 = (bf16[2,128,128]{2,1,0:T(8,128)(2,1)S(1)}, bf16[2,128,128]{2,1,0:T(8,128)(2,1)S(1)}, u32[]{:S(2)}, u32[]{:S(2)}) collective-permute-start(bf16[2,128,128]{2,1,0:T(8,128)(2,1)S(1)} %fusion.33), channel_id=1, source_target_pairs={{8,0},{16,8},{24,16},{32,24},{40,32},{48,40},{56,48},{64,56},{72,6... | collective-permute-start | bytes 196616 | tf_op jit(solution)/shard_map/while/body/eval_jaxpr/ppermute | solution.py:16
  375.1 11.4 %collective-permute-start.1 = (bf16[2,128,128]{2,1,0:T(8,128)(2,1)S(1)}, bf16[2,128,128]{2,1,0:T(8,128)(2,1)S(1)}, u32[]{:S(2)}, u32[]{:S(2)}) collective-permute-start(bf16[2,128,128]{2,1,0:T(8,128)(2,1)S(1)} %fusion.33), channel_id=1, source_target_pairs={{8,0},{16,8},{24,16},{32,24},{40,32},{48,40},{56,48},{64,56},{72,6... | collective-permute-start | bytes 196616 | tf_op jit(solution)/shard_map/while/body/eval_jaxpr/ppermute | solution.py:16
  387.5 11.3 %collective-permute-start.1 = (bf16[2,128,128]{2,1,0:T(8,128)(2,1)S(1)}, bf16[2,128,128]{2,1,0:T(8,128)(2,1)S(1)}, u32[]{:S(2)}, u32[]{:S(2)}) collective-permute-start(bf16[2,128,128]{2,1,0:T(8,128)(2,1)S(1)} %fusion.33), channel_id=1, source_target_pairs={{8,0},{16,8},{24,16},{32,24},{40,32},{48,40},{56,48},{64,56},{72,6... | collective-permute-start | bytes 196616 | tf_op jit(solution)/shard_map/while/body/eval_jaxpr/ppermute | solution.py:16
  399.8 11.3 %collective-permute-start.1 = (bf16[2,128,128]{2,1,0:T(8,128)(2,1)S(1)}, bf16[2,128,128]{2,1,0:T(8,128)(2,1)S(1)}, u32[]{:S(2)}, u32[]{:S(2)}) collective-permute-start(bf16[2,128,128]{2,1,0:T(8,128)(2,1)S(1)} %fusion.33), channel_id=1, source_target_pairs={{8,0},{16,8},{24,16},{32,24},{40,32},{48,40},{56,48},{64,56},{72,6... | collective-permute-start | bytes 196616 | tf_op jit(solution)/shard_map/while/body/eval_jaxpr/ppermute | solution.py:16
  412.0 11.3 %collective-permute-start.1 = (bf16[2,128,128]{2,1,0:T(8,128)(2,1)S(1)}, bf16[2,128,128]{2,1,0:T(8,128)(2,1)S(1)}, u32[]{:S(2)}, u32[]{:S(2)}) collective-permute-start(bf16[2,128,128]{2,1,0:T(8,128)(2,1)S(1)} %fusion.33), channel_id=1, source_target_pairs={{8,0},{16,8},{24,16},{32,24},{40,32},{48,40},{56,48},{64,56},{72,6... | collective-permute-start | bytes 196616 | tf_op jit(solution)/shard_map/while/body/eval_jaxpr/ppermute | solution.py:16
  424.3 11.3 %collective-permute-start.1 = (bf16[2,128,128]{2,1,0:T(8,128)(2,1)S(1)}, bf16[2,128,128]{2,1,0:T(8,128)(2,1)S(1)}, u32[]{:S(2)}, u32[]{:S(2)}) collective-permute-start(bf16[2,128,128]{2,1,0:T(8,128)(2,1)S(1)} %fusion.33), channel_id=1, source_target_pairs={{8,0},{16,8},{24,16},{32,24},{40,32},{48,40},{56,48},{64,56},{72,6... | collective-permute-start | bytes 196616 | tf_op jit(solution)/shard_map/while/body/eval_jaxpr/ppermute | solution.py:16
  436.5 11.3 %collective-permute-start.1 = (bf16[2,128,128]{2,1,0:T(8,128)(2,1)S(1)}, bf16[2,128,128]{2,1,0:T(8,128)(2,1)S(1)}, u32[]{:S(2)}, u32[]{:S(2)}) collective-permute-start(bf16[2,128,128]{2,1,0:T(8,128)(2,1)S(1)} %fusion.33), channel_id=1, source_target_pairs={{8,0},{16,8},{24,16},{32,24},{40,32},{48,40},{56,48},{64,56},{72,6... | collective-permute-start | bytes 196616 | tf_op jit(solution)/shard_map/while/body/eval_jaxpr/ppermute | solution.py:16
  448.8 11.3 %collective-permute-start.1 = (bf16[2,128,128]{2,1,0:T(8,128)(2,1)S(1)}, bf16[2,128,128]{2,1,0:T(8,128)(2,1)S(1)}, u32[]{:S(2)}, u32[]{:S(2)}) collective-permute-start(bf16[2,128,128]{2,1,0:T(8,128)(2,1)S(1)} %fusion.33), channel_id=1, source_target_pairs={{8,0},{16,8},{24,16},{32,24},{40,32},{48,40},{56,48},{64,56},{72,6... | collective-permute-start | bytes 196616 | tf_op jit(solution)/shard_map/while/body/eval_jaxpr/ppermute | solution.py:16
  461.0 11.3 %collective-permute-start.1 = (bf16[2,128,128]{2,1,0:T(8,128)(2,1)S(1)}, bf16[2,128,128]{2,1,0:T(8,128)(2,1)S(1)}, u32[]{:S(2)}, u32[]{:S(2)}) collective-permute-start(bf16[2,128,128]{2,1,0:T(8,128)(2,1)S(1)} %fusion.33), channel_id=1, source_target_pairs={{8,0},{16,8},{24,16},{32,24},{40,32},{48,40},{56,48},{64,56},{72,6... | collective-permute-start | bytes 196616 | tf_op jit(solution)/shard_map/while/body/eval_jaxpr/ppermute | solution.py:16
  473.2 11.5 %collective-permute-start.1 = (bf16[2,128,128]{2,1,0:T(8,128)(2,1)S(1)}, bf16[2,128,128]{2,1,0:T(8,128)(2,1)S(1)}, u32[]{:S(2)}, u32[]{:S(2)}) collective-permute-start(bf16[2,128,128]{2,1,0:T(8,128)(2,1)S(1)} %fusion.33), channel_id=1, source_target_pairs={{8,0},{16,8},{24,16},{32,24},{40,32},{48,40},{56,48},{64,56},{72,6... | collective-permute-start | bytes 196616 | tf_op jit(solution)/shard_map/while/body/eval_jaxpr/ppermute | solution.py:16
  485.7 11.4 %collective-permute-start.1 = (bf16[2,128,128]{2,1,0:T(8,128)(2,1)S(1)}, bf16[2,128,128]{2,1,0:T(8,128)(2,1)S(1)}, u32[]{:S(2)}, u32[]{:S(2)}) collective-permute-start(bf16[2,128,128]{2,1,0:T(8,128)(2,1)S(1)} %fusion.33), channel_id=1, source_target_pairs={{8,0},{16,8},{24,16},{32,24},{40,32},{48,40},{56,48},{64,56},{72,6... | collective-permute-start | bytes 196616 | tf_op jit(solution)/shard_map/while/body/eval_jaxpr/ppermute | solution.py:16
  498.1 11.3 %collective-permute-start.1 = (bf16[2,128,128]{2,1,0:T(8,128)(2,1)S(1)}, bf16[2,128,128]{2,1,0:T(8,128)(2,1)S(1)}, u32[]{:S(2)}, u32[]{:S(2)}) collective-permute-start(bf16[2,128,128]{2,1,0:T(8,128)(2,1)S(1)} %fusion.33), channel_id=1, source_target_pairs={{8,0},{16,8},{24,16},{32,24},{40,32},{48,40},{56,48},{64,56},{72,6... | collective-permute-start | bytes 196616 | tf_op jit(solution)/shard_map/while/body/eval_jaxpr/ppermute | solution.py:16
  510.4 11.3 %collective-permute-start.1 = (bf16[2,128,128]{2,1,0:T(8,128)(2,1)S(1)}, bf16[2,128,128]{2,1,0:T(8,128)(2,1)S(1)}, u32[]{:S(2)}, u32[]{:S(2)}) collective-permute-start(bf16[2,128,128]{2,1,0:T(8,128)(2,1)S(1)} %fusion.33), channel_id=1, source_target_pairs={{8,0},{16,8},{24,16},{32,24},{40,32},{48,40},{56,48},{64,56},{72,6... | collective-permute-start | bytes 196616 | tf_op jit(solution)/shard_map/while/body/eval_jaxpr/ppermute | solution.py:16
  522.6 11.3 %collective-permute-start.1 = (bf16[2,128,128]{2,1,0:T(8,128)(2,1)S(1)}, bf16[2,128,128]{2,1,0:T(8,128)(2,1)S(1)}, u32[]{:S(2)}, u32[]{:S(2)}) collective-permute-start(bf16[2,128,128]{2,1,0:T(8,128)(2,1)S(1)} %fusion.33), channel_id=1, source_target_pairs={{8,0},{16,8},{24,16},{32,24},{40,32},{48,40},{56,48},{64,56},{72,6... | collective-permute-start | bytes 196616 | tf_op jit(solution)/shard_map/while/body/eval_jaxpr/ppermute | solution.py:16
  534.9 11.3 %collective-permute-start.1 = (bf16[2,128,128]{2,1,0:T(8,128)(2,1)S(1)}, bf16[2,128,128]{2,1,0:T(8,128)(2,1)S(1)}, u32[]{:S(2)}, u32[]{:S(2)}) collective-permute-start(bf16[2,128,128]{2,1,0:T(8,128)(2,1)S(1)} %fusion.33), channel_id=1, source_target_pairs={{8,0},{16,8},{24,16},{32,24},{40,32},{48,40},{56,48},{64,56},{72,6... | collective-permute-start | bytes 196616 | tf_op jit(solution)/shard_map/while/body/eval_jaxpr/ppermute | solution.py:16
  547.1 11.3 %collective-permute-start.1 = (bf16[2,128,128]{2,1,0:T(8,128)(2,1)S(1)}, bf16[2,128,128]{2,1,0:T(8,128)(2,1)S(1)}, u32[]{:S(2)}, u32[]{:S(2)}) collective-permute-start(bf16[2,128,128]{2,1,0:T(8,128)(2,1)S(1)} %fusion.33), channel_id=1, source_target_pairs={{8,0},{16,8},{24,16},{32,24},{40,32},{48,40},{56,48},{64,56},{72,6... | collective-permute-start | bytes 196616 | tf_op jit(solution)/shard_map/while/body/eval_jaxpr/ppermute | solution.py:16
  559.4 11.3 %collective-permute-start.1 = (bf16[2,128,128]{2,1,0:T(8,128)(2,1)S(1)}, bf16[2,128,128]{2,1,0:T(8,128)(2,1)S(1)}, u32[]{:S(2)}, u32[]{:S(2)}) collective-permute-start(bf16[2,128,128]{2,1,0:T(8,128)(2,1)S(1)} %fusion.33), channel_id=1, source_target_pairs={{8,0},{16,8},{24,16},{32,24},{40,32},{48,40},{56,48},{64,56},{72,6... | collective-permute-start | bytes 196616 | tf_op jit(solution)/shard_map/while/body/eval_jaxpr/ppermute | solution.py:16
  571.6 11.3 %collective-permute-start.1 = (bf16[2,128,128]{2,1,0:T(8,128)(2,1)S(1)}, bf16[2,128,128]{2,1,0:T(8,128)(2,1)S(1)}, u32[]{:S(2)}, u32[]{:S(2)}) collective-permute-start(bf16[2,128,128]{2,1,0:T(8,128)(2,1)S(1)} %fusion.33), channel_id=1, source_target_pairs={{8,0},{16,8},{24,16},{32,24},{40,32},{48,40},{56,48},{64,56},{72,6... | collective-permute-start | bytes 196616 | tf_op jit(solution)/shard_map/while/body/eval_jaxpr/ppermute | solution.py:16
  583.8 11.3 %collective-permute-start.1 = (bf16[2,128,128]{2,1,0:T(8,128)(2,1)S(1)}, bf16[2,128,128]{2,1,0:T(8,128)(2,1)S(1)}, u32[]{:S(2)}, u32[]{:S(2)}) collective-permute-start(bf16[2,128,128]{2,1,0:T(8,128)(2,1)S(1)} %fusion.33), channel_id=1, source_target_pairs={{8,0},{16,8},{24,16},{32,24},{40,32},{48,40},{56,48},{64,56},{72,6... | collective-permute-start | bytes 196616 | tf_op jit(solution)/shard_map/while/body/eval_jaxpr/ppermute | solution.py:16
  596.1 11.8 %collective-permute-start.1 = (bf16[2,128,128]{2,1,0:T(8,128)(2,1)S(1)}, bf16[2,128,128]{2,1,0:T(8,128)(2,1)S(1)}, u32[]{:S(2)}, u32[]{:S(2)}) collective-permute-start(bf16[2,128,128]{2,1,0:T(8,128)(2,1)S(1)} %fusion.33), channel_id=1, source_target_pairs={{8,0},{16,8},{24,16},{32,24},{40,32},{48,40},{56,48},{64,56},{72,6... | collective-permute-start | bytes 196616 | tf_op jit(solution)/shard_map/while/body/eval_jaxpr/ppermute | solution.py:16
  608.9 11.4 %collective-permute-start.1 = (bf16[2,128,128]{2,1,0:T(8,128)(2,1)S(1)}, bf16[2,128,128]{2,1,0:T(8,128)(2,1)S(1)}, u32[]{:S(2)}, u32[]{:S(2)}) collective-permute-start(bf16[2,128,128]{2,1,0:T(8,128)(2,1)S(1)} %fusion.33), channel_id=1, source_target_pairs={{8,0},{16,8},{24,16},{32,24},{40,32},{48,40},{56,48},{64,56},{72,6... | collective-permute-start | bytes 196616 | tf_op jit(solution)/shard_map/while/body/eval_jaxpr/ppermute | solution.py:16
  621.2 11.3 %collective-permute-start.1 = (bf16[2,128,128]{2,1,0:T(8,128)(2,1)S(1)}, bf16[2,128,128]{2,1,0:T(8,128)(2,1)S(1)}, u32[]{:S(2)}, u32[]{:S(2)}) collective-permute-start(bf16[2,128,128]{2,1,0:T(8,128)(2,1)S(1)} %fusion.33), channel_id=1, source_target_pairs={{8,0},{16,8},{24,16},{32,24},{40,32},{48,40},{56,48},{64,56},{72,6... | collective-permute-start | bytes 196616 | tf_op jit(solution)/shard_map/while/body/eval_jaxpr/ppermute | solution.py:16
  633.5 11.3 %collective-permute-start.1 = (bf16[2,128,128]{2,1,0:T(8,128)(2,1)S(1)}, bf16[2,128,128]{2,1,0:T(8,128)(2,1)S(1)}, u32[]{:S(2)}, u32[]{:S(2)}) collective-permute-start(bf16[2,128,128]{2,1,0:T(8,128)(2,1)S(1)} %fusion.33), channel_id=1, source_target_pairs={{8,0},{16,8},{24,16},{32,24},{40,32},{48,40},{56,48},{64,56},{72,6... | collective-permute-start | bytes 196616 | tf_op jit(solution)/shard_map/while/body/eval_jaxpr/ppermute | solution.py:16
Sparse Core Ops, SparseCore 0:
  337.5 39.8 reduce-scatter.3
where the time goes:
time: 657 us; the launch traced here: 655 us
  waiting for transfers between devices  274 us (42%)
  starting transfers between devices  265 us (40%)
  local copies, waits for them, and re-layouts  33.1 us (5%)
  other arithmetic  31.7 us (5%)
  blocking collectives  21.5 us (3%)
  between operations  14.2 us (2%)
  matrix products  14 us (2%)
    ppermute x48, waiting for transfers between devices, from_behind(): lax.ppermute(value, axis, [(source, source + steps) for source in range(f...  274 us
    ppermute x48, starting transfers between devices, from_behind(): lax.ppermute(value, axis, [(source, source + steps) for source in range(f...  265 us
    convert_element_type x24, other arithmetic, carry_against(): collected.astype(jnp.bfloat16)  22.3 us
    all_gather x1, blocking collectives, shards(): lax.all_gather(out_grad, 'head', axis=1, tiled=True)  21.5 us
    dynamic_update_slice x24, local copies, waits for them, and re-layouts, collect(): stored = lax.dynamic_update_index_in_dim(stored, moving, step_num, 0)  14.9 us
  transfers between devices with their start and end apart: 49, of which 48 were waited for; matrix products, arithmetic and copies ran while one was open for 6% of the time, Pallas kernels for 0%

commit v1 on v0

v1 whole, which is shorter than its diff:
```python
import math

import jax
import jax.numpy as jnp
from jax import lax
from jax.experimental import pallas as pl
from jax.experimental.pallas import tpu as pltpu
from jax.sharding import PartitionSpec as P

HD = 128
GROUP = 3
TOK = 128
LO = 3
LINKS = 32
REACH = 8
N_SEQ = LO * LINKS
N_HEAD = 8
N_HI = 4
WIDTH = GROUP * HD
BUNDLE = LO * TOK
SCALE = 1.0 / math.sqrt(HD)
EXP2_SCALE = SCALE * math.log2(math.e)
MASKED = -1e30
MESH = pl.DeviceIdType.MESH
F32 = jnp.float32
BF16 = jnp.bfloat16


def mm(a, b):
    return jnp.dot(a, b, preferred_element_type=F32)


def mm_t(a, b):
    return lax.dot_general(a, b, (((1,), (1,)), ((), ())), preferred_element_type=F32)


def blocks_t(x):
    if x.shape[0] == HD:
        return jnp.concatenate([x[:, i * HD:(i + 1) * HD].T for i in range(GROUP)], axis=0)
    return jnp.concatenate([x[i * HD:(i + 1) * HD, :].T for i in range(GROUP)], axis=1)


def kernel(
    clip_ref, q_ref, k_ref, v_ref, og_ref, w_hbm,
    mixed_ref, att_ref, dq_ref, dk_ref, dv_ref,
    kv, og, w, qt, qs, dot, dos, start, s_buf, p_buf, kt, vt, mx, acc,
    part, psib, pmine, pfar, up_in, down_in, stage, zs, zr,
    w_sem, kv_send, kv_recv, og_send, og_recv, osib_send, osib_recv,
    part_send, part_recv, pfar_send, pfar_recv,
    up_send, up_recv, down_send, down_recv, z_send, z_recv,
):
    s = lax.axis_index("seq")
    n = lax.axis_index("head")
    link, z = lax.div(s, LO), lax.rem(s, LO)
    hi, core = lax.div(n, 2), lax.rem(n, 2)

    def at_link(step):
        return (lax.rem(s + step * LO + N_SEQ, N_SEQ), n)

    def at_lo(r):
        return (link * LO + lax.rem(z + r, LO), n)

    def at_hi(d):
        return (s, lax.rem(hi + d, N_HI) * 2 + core)

    sibling = (s, hi * 2 + 1 - core)
    lo_of = [lax.rem(z + LO - r, LO) for r in range(LO)]

    def copy(src, dst, ssem, rsem, dev):
        return pltpu.make_async_remote_copy(
            src_ref=src, dst_ref=dst, send_sem=ssem, recv_sem=rsem, device_id=dev, device_id_type=MESH
        )

    sent = []

    def go(c):
        c.start()
        sent.append(c)

    w_copy = pltpu.make_async_copy(w_hbm, w, w_sem)
    w_copy.start()
    kv[0, z, 0] = k_ref[...]
    kv[0, z, 1] = v_ref[...]
    og[n] = og_ref[...]

    barrier = pltpu.get_barrier_semaphore()
    partners = [at_link(1), at_link(-1), at_link(REACH), at_link(-REACH), at_lo(1), at_lo(2)]
    partners += [sibling] + [at_hi(d) for d in (1, 2, 3)]
    for dev in partners:
        pl.semaphore_signal(barrier, inc=1, device_id=dev, device_id_type=MESH)
    pl.semaphore_wait(barrier, len(partners))

    def z_copy(r):
        return copy(kv.at[0, z], kv.at[0, z], kv_send.at[0, r], kv_recv.at[0, r], at_lo(r))

    def up_copy(k, r):
        return copy(kv.at[k - 1, lo_of[r]], kv.at[k, lo_of[r]], kv_send.at[k, r], kv_recv.at[k, r], at_link(1))

    def down_copy(k, r):
        if k == REACH:
            return copy(kv.at[0, lo_of[r]], kv.at[k, lo_of[r]], kv_send.at[k, r], kv_recv.at[k, r], at_link(REACH))
        return copy(kv.at[k + 1, lo_of[r]], kv.at[k, lo_of[r]], kv_send.at[k, r], kv_recv.at[k, r], at_link(-1))

    def og_copy(d):
        return copy(og.at[n], og.at[n], og_send.at[d], og_recv.at[d], at_hi(d))

    def sib_copy(d):
        m = lax.rem(hi + N_HI - d, N_HI) * 2 + core
        return copy(og.at[m], og.at[m], osib_send.at[d], osib_recv.at[d], sibling)

    go(up_copy(1, 0))
    go(down_copy(REACH, 0))
    for r in (1, 2):
        go(z_copy(r))
    for d in (2, 1, 3):
        go(og_copy(d))
    go(sib_copy(0))

    q_t = jnp.concatenate([q_ref[:, i * HD:(i + 1) * HD].astype(F32).T for i in range(GROUP)], axis=1)
    qt[...] = q_t.astype(BF16)
    lane = lax.broadcasted_iota(jnp.int32, (1, WIDTH), 1)
    pos = s * TOK + lax.rem(lane, TOK)
    begin = jnp.zeros_like(pos)
    end = jnp.int32(0)
    for i in range(8):
        end = end + clip_ref[i]
        begin = jnp.where(pos >= end, end, begin)
    start[...] = jnp.broadcast_to(begin, start.shape)

    for r in (1, 2):
        z_copy(r).wait_recv()
        go(up_copy(1, r))
        go(down_copy(REACH, r))

    def scores(k, first=False):
        keys = kv[k, :, 0].reshape(BUNDLE, HD)
        sc = mm(keys, qt[...])
        row = (link - k) * BUNDLE + lax.broadcasted_iota(jnp.int32, (BUNDLE, WIDTH), 0)
        ok = row >= start[0:1, :]
        if k == 0:
            ok = ok & (row <= pos)
        sc = jnp.where(ok, sc, MASKED)
        s_buf[k] = sc
        top = jnp.max(sc.reshape(BUNDLE // 8, 8, WIDTH), axis=0)
        mx[...] = top if first else jnp.maximum(mx[...], top)
        for i in range(LO):
            cols = slice(k * BUNDLE + i * TOK, k * BUNDLE + (i + 1) * TOK)
            kt[:, cols] = kv[k, i, 0].T
            vt[:, cols] = kv[k, i, 1].T

    scores(0, True)
    for step in range(1, 5):
        up, down = step, REACH + 1 - step
        for r in range(LO):
            up_copy(up, r).wait_recv()
            if step < 4:
                go(up_copy(up + 1, r))
            down_copy(down, r).wait_recv()
            if step < 4:
                go(down_copy(down - 1, r))
        if step == 2:
            for d in (1, 3):
                og_copy(d).wait_recv()
                go(sib_copy(d))
        if step == 3:
            og_copy(2).wait_recv()
            go(sib_copy(2))
        scores(up)
        scores(down)

    w_copy.wait()
    for d in range(N_HI):
        sib_copy(d).wait_recv()
    dh = mm_t(w[:, 0:WIDTH], og[0])
    for m in range(1, N_HEAD):
        dh = dh + mm_t(w[:, m * WIDTH:(m + 1) * WIDTH], og[m])
    dh_t = jnp.concatenate([dh[i * HD:(i + 1) * HD, :] for i in range(GROUP)], axis=1)
    dot[...] = dh_t.astype(BF16)

    top = jnp.max(mx[...], axis=0, keepdims=True) * EXP2_SCALE
    total = jnp.zeros((8, WIDTH), F32)
    for k in range(REACH + 1):
        p = jnp.exp2(s_buf[k] * EXP2_SCALE - top)
        total = total + jnp.sum(p.reshape(BUNDLE // 8, 8, WIDTH), axis=0)
        p_buf[k * BUNDLE:(k + 1) * BUNDLE, :] = p.astype(BF16)
    inv = 1.0 / jnp.sum(total, axis=0, keepdims=True)
    out_t = (mm(vt[...], p_buf[...]) * inv).astype(BF16).astype(F32)
    attended = jnp.concatenate([out_t[:, i * HD:(i + 1) * HD].T for i in range(GROUP)], axis=1).astype(BF16)
    att_ref[...] = attended
    d_t = dot[...].astype(F32)
    delta = jnp.sum(d_t * out_t, axis=0, keepdims=True)
    dos[...] = blocks_t(d_t * inv).astype(BF16)
    qs[...] = blocks_t(qt[...].astype(F32) * (inv * SCALE)).astype(BF16)

    def backward(k):
        rows = slice(k * BUNDLE, (k + 1) * BUNDLE)
        p = p_buf[rows, :]
        dp = mm(kv[k, :, 1].reshape(BUNDLE, HD), dot[...])
        ds = (p.astype(F32) * (dp - delta)).astype(BF16)
        acc[1] = mm(p, dos[...]).reshape(LO, TOK, HD)
        acc[0] = mm(ds, qs[...]).reshape(LO, TOK, HD)
        p_buf[rows, :] = ds

    def up_back(k, i):
        return copy(stage.at[k, i], up_in.at[k - 1, i], up_send.at[k - 1, i], up_recv.at[k - 1, i], at_link(-1))

    def down_back(k, i):
        dev = at_link(-REACH) if k == REACH else at_link(1)
        return copy(stage.at[k, i], down_in.at[k - 5, i], down_send.at[k - 5, i], down_recv.at[k - 5, i], dev)

    def send_up(k):
        backward(k)
        for i in range(LO):
            total = acc[:, i]
            if k < 4:
                up_back(k + 1, i).wait_recv()
                total = total + up_in[k, i].astype(F32)
            stage[k, i] = total.astype(BF16)
            go(up_back(k, i))

    def send_down(k):
        backward(k)
        for i in range(LO):
            total = acc[:, i]
            if k > 5:
                down_back(k - 1, i).wait_recv()
                total = total + down_in[k - 6, i].astype(F32)
            stage[k, i] = total.astype(BF16)
            go(down_back(k, i))

    send_up(4)
    send_down(5)

    def part_copy(d):
        m = lax.rem(hi + d, N_HI) * 2 + 1 - core
        return copy(part.at[m], psib.at[d], part_send.at[d], part_recv.at[d], sibling)

    def far_copy(d):
        return copy(pmine.at[d], pfar.at[d], pfar_send.at[d], pfar_recv.at[d], at_hi(d))

    for m in range(N_HEAD):
        part[m] = mm(attended, w[:, m * WIDTH:(m + 1) * WIDTH]).astype(BF16)
    for d in (2, 1, 3, 0):
        go(part_copy(d))

    send_up(3)
    send_down(6)

    for d in (2, 1, 3, 0):
        part_copy(d).wait_recv()
        m = lax.rem(hi + d, N_HI) * 2 + core
        both = part[m].astype(F32) + psib[d].astype(F32)
        pmine[d] = both.astype(BF16)
        if d:
            go(far_copy(d))

    send_up(2)
    send_down(7)
    send_up(1)
    send_down(8)
    backward(0)
    for i in range(LO):
        up_back(1, i).wait_recv()
        down_back(8, i).wait_recv()
        zs[i] = (acc[:, i] + up_in[0, i].astype(F32) + down_in[3, i].astype(F32)).astype(BF16)

    def z_back(r):
        return copy(zs.at[lax.rem(z + r, LO)], zr.at[r - 1], z_send.at[r - 1], z_recv.at[r - 1], at_lo(r))

    for r in (1, 2):
        go(z_back(r))

    dq_t = mm(kt[...], p_buf[...]) * (inv * SCALE)
    dq_ref[...] = jnp.concatenate([dq_t[:, i * HD:(i + 1) * HD].T for i in range(GROUP)], axis=1).astype(BF16)

    for d in (1, 2, 3):
        far_copy(d).wait_recv()
    mixed_ref[...] = (
        pmine[0].astype(F32) + pfar[1].astype(F32) + pfar[2].astype(F32) + pfar[3].astype(F32)
    ).astype(BF16)

    for r in (1, 2):
        z_back(r).wait_recv()
    mine = zs[z].astype(F32) + zr[0].astype(F32) + zr[1].astype(F32)
    dk_ref[...] = mine[0].astype(BF16)
    dv_ref[...] = mine[1].astype(BF16)

    for c in sent:
        c.wait_send()


def shards(query_heads, key_heads, value_heads, out_weight, out_grad, clip_lengths):
    dma = pltpu.SemaphoreType.DMA
    vmem = pltpu.VMEM
    keys = (REACH + 1) * BUNDLE
    whole = pl.BlockSpec(memory_space=pltpu.VMEM)
    block = jax.ShapeDtypeStruct((TOK, WIDTH), BF16)
    small = jax.ShapeDtypeStruct((TOK, HD), BF16)
    piece = (2, TOK, HD)
    return pl.pallas_call(
        kernel,
        out_shape=(block, block, block, small, small),
        in_specs=[pl.BlockSpec(memory_space=pltpu.SMEM)] + [whole] * 4 + [pl.BlockSpec(memory_space=pl.ANY)],
        out_specs=[whole] * 5,
        scratch_shapes=[
            vmem((REACH + 1, LO) + piece, BF16),
            vmem((N_HEAD, TOK, WIDTH), BF16),
            vmem((WIDTH, N_HEAD * WIDTH), BF16),
            vmem((HD, WIDTH), BF16),
            vmem((WIDTH, HD), BF16),
            vmem((HD, WIDTH), BF16),
            vmem((WIDTH, HD), BF16),
            vmem((8, WIDTH), jnp.int32),
            vmem((REACH + 1, BUNDLE, WIDTH), F32),
            vmem((keys, WIDTH), BF16),
            vmem((HD, keys), BF16),
            vmem((HD, keys), BF16),
            vmem((8, WIDTH), F32),
            vmem((2, LO, TOK, HD), F32),
            vmem((N_HEAD, TOK, WIDTH), BF16),
            vmem((N_HI, TOK, WIDTH), BF16),
            vmem((N_HI, TOK, WIDTH), BF16),
            vmem((N_HI, TOK, WIDTH), BF16),
            vmem((4, LO) + piece, BF16),
            vmem((4, LO) + piece, BF16),
            vmem((REACH + 1, LO) + piece, BF16),
            vmem((LO,) + piece, BF16),
            vmem((LO - 1,) + piece, BF16),
            dma,
            dma((REACH + 1, LO)), dma((REACH + 1, LO)),
            dma((N_HI,)), dma((N_HI,)), dma((N_HI,)), dma((N_HI,)),
            dma((N_HI,)), dma((N_HI,)), dma((N_HI,)), dma((N_HI,)),
            dma((4, LO)), dma((4, LO)), dma((4, LO)), dma((4, LO)),
            dma((LO - 1,)), dma((LO - 1,)),
        ],
        compiler_params=pltpu.CompilerParams(
            collective_id=0, has_side_effects=True, vmem_limit_bytes=48 * 1024 * 1024
        ),
        cost_estimate=pl.CostEstimate(flops=3_000_000_000, bytes_accessed=4_000_000, transcendentals=1_400_000),
    )(clip_lengths, query_heads, key_heads, value_heads, out_grad, out_weight)


def solution(mesh):
    wide = P("seq", "head")
    return jax.shard_map(
        shards,
        mesh=mesh,
        in_specs=(wide, wide, wide, P("head", None), wide, P()),
        out_specs=(wide,) * 5,
        check_vma=False,
    )
```

time: 657 us -> 90.2 us (0.14)
  the two profiles are of different devices: /device:TPU:196 before, /device:TPU:198 now
where the time goes in v1:
time: 90.2 us; the launch traced here: 89.8 us
  Pallas kernels  80.4 us (89%)
  local copies, waits for them, and re-layouts  8.76 us (10%)
    pallas_call x1, Pallas kernels, shards(): pl.pallas_call(kernel, out_shape=(block, block, block, small, small), in_...  80.4 us
    unnamed x17, local copies, waits for them, and re-layouts  8.76 us

profile of v1, /device:TPU:198, one launch (start us, length us, event | category | flops | bytes accessed | tf_op | source)
XLA Modules:
  0.0 89.8 jit_solution(1296207800661658513)
XLA Ops:
  0.6 0.0 copy-start
  0.6 1.7 %copy-done = bf16[384,3072]{1,0:T(8,128)(2,1)S(1)} copy-done((bf16[384,3072]{1,0:T(8,128)(2,1)S(1)}, bf16[384,3072]{1,0:T(8,128)(2,1)}, u32[]{:S(2)}) %copy-start) | copy-done | bytes 2359320
  2.3 0.0 copy-start.1
  2.3 0.9 copy-done.1
  3.2 0.0 copy-start.2
  3.2 0.9 copy-done.2
  4.1 0.0 copy-start.3
  4.1 0.8 copy-done.3
  4.8 0.0 copy-start.4
  4.8 0.8 copy-done.4
  5.6 0.0 copy-start.5
  5.6 0.7 copy-done.5
  6.3 80.4 %shard_map.101 = (bf16[128,384]{1,0:T(8,128)(2,1)S(1)}, bf16[128,384]{1,0:T(8,128)(2,1)S(1)}, bf16[128,384]{1,0:T(8,128)(2,1)S(1)}, bf16[128,128]{1,0:T(8,128)(2,1)S(1)}, bf16[128,128]{1,0:T(8,128)(2,1)S(1)}) custom-call(s32[8]{0:T(128)S(1)} %copy-done.5, bf16[128,384]{1,0:T(8,128)(2,1)S(1)} %copy-done.1, bf16[128,128]{1,0:T(8,128)(2,1)S(1)} %copy-done.3, ...), custom_call_target="tpu_custom_call" | custom-call | flops 3000000000 | bytes 4000000 | tf_op jit(solution)/shard_map/pallas_call | solution.py:300
  86.7 0.6 copy.16
  87.3 0.6 copy.17
  88.0 0.6 copy.18
  88.6 0.6 copy.19
  89.2 0.6 copy.20
Async XLA Ops:
  0.6 1.7 %copy-start = (bf16[384,3072]{1,0:T(8,128)(2,1)S(1)}, bf16[384,3072]{1,0:T(8,128)(2,1)}, u32[]{:S(2)}) copy-start(bf16[384,3072]{1,0:T(8,128)(2,1)} %w_hbm.1) | copy-start | bytes 7077892
  2.3 0.9 copy-start.1
  3.2 0.9 copy-start.2
  4.1 0.8 copy-start.3
  4.8 0.8 copy-start.4
  5.6 0.7 copy-start.5

commit v2 on v1

v2 whole, which is shorter than its diff:
```python
import math

import jax
import jax.numpy as jnp
from jax import lax
from jax.experimental import pallas as pl
from jax.experimental.pallas import tpu as pltpu
from jax.sharding import PartitionSpec as P

HD = 128
GROUP = 3
TOK = 128
LO = 3
LINKS = 32
RING = 8
N_SEQ = LO * LINKS
N_HEAD = 8
N_HI = 4
WIDTH = GROUP * HD
BUNDLE = LO * TOK
SCALE = 1.0 / math.sqrt(HD)
EXP2_SCALE = SCALE * math.log2(math.e)
MASKED = -1e30
MESH = pl.DeviceIdType.MESH
F32 = jnp.float32
BF16 = jnp.bfloat16


def mm(a, b):
    return jnp.dot(a, b, preferred_element_type=F32)


def mm_t(a, b):
    return lax.dot_general(a, b, (((1,), (1,)), ((), ())), preferred_element_type=F32)


def blocks_t(x):
    if x.shape[0] == HD:
        return jnp.concatenate([x[:, i * HD:(i + 1) * HD].T for i in range(GROUP)], axis=0)
    return jnp.concatenate([x[i * HD:(i + 1) * HD, :].T for i in range(GROUP)], axis=1)


def kernel(
    clip_ref, q_hbm, k_hbm, v_hbm, og_hbm, w_hbm,
    mixed_hbm, att_hbm, dq_hbm, dk_hbm, dv_hbm,
    q_in, kv, og, w, qt, qs, dot, dos, s_buf, p_buf, kt, vt, mx, acc,
    part, psib, pmine, pfar, up_in, down_in, stage, zs, zr,
    mixed_ref, att_ref, dq_ref, dk_ref, dv_ref,
    in_sem, out_sem, ready,
    kv_send, kv_recv, og_send, og_recv, osib_send, osib_recv,
    part_send, part_recv, pfar_send, pfar_recv,
    up_send, up_recv, down_send, down_recv, z_send, z_recv,
):
    s = lax.axis_index("seq")
    n = lax.axis_index("head")
    link, z = lax.div(s, LO), lax.rem(s, LO)
    hi, core = lax.div(n, 2), lax.rem(n, 2)
    y = lax.rem(link, RING)
    last, inner = y == RING - 1, y < RING - 1

    def at_seq(step):
        return (lax.rem(s + step + N_SEQ, N_SEQ), n)

    def at_link(step):
        return at_seq(step * LO)

    def at_lo(r):
        return (link * LO + lax.rem(z + r, LO), n)

    def at_hi(d):
        return (s, lax.rem(hi + d, N_HI) * 2 + core)

    sibling = (s, hi * 2 + 1 - core)
    lo_of = [lax.rem(z + LO - r, LO) for r in range(LO)]

    def copy(src, dst, ssem, rsem, dev):
        return pltpu.make_async_remote_copy(
            src_ref=src, dst_ref=dst, send_sem=ssem, recv_sem=rsem, device_id=dev, device_id_type=MESH
        )

    sent = []

    def go(c):
        c.start()
        sent.append(c)

    def go_if(cond, c):
        pl.when(cond)(c.start)

    def load(i, src, dst):
        c = pltpu.make_async_copy(src, dst, in_sem.at[i])
        c.start()
        return c

    loads = [
        load(0, k_hbm, kv.at[0, z, 0]), load(1, v_hbm, kv.at[0, z, 1]),
        load(2, og_hbm, og.at[n]), load(3, q_hbm, q_in), load(4, w_hbm, w),
    ]

    barrier = pltpu.get_barrier_semaphore()
    near = [at_link(1), at_link(-1), at_link(RING), at_link(-RING), at_lo(1), at_lo(2), sibling]
    for dev in near:
        pl.semaphore_signal(barrier, inc=1, device_id=dev, device_id_type=MESH)

    def greet(cond, dev, sem):
        @pl.when(cond)
        def _():
            pl.semaphore_signal(sem, inc=1, device_id=dev, device_id_type=MESH)

    greet(last, at_seq(-(RING - 1) * LO), barrier)
    greet(y == 0, at_seq((RING - 1) * LO), barrier)
    for d in (1, 2, 3):
        greet(hi + d < N_HI, at_hi(d), barrier)
    ends = jnp.where(last | (y == 0), 1, 0)
    pl.semaphore_wait(barrier, len(near) + hi + ends)
    for d in (1, 2, 3):
        greet(hi + d >= N_HI, at_hi(d), ready.at[N_HI - d])

    def z_copy(r):
        return copy(kv.at[0, z], kv.at[0, z], kv_send.at[0, r], kv_recv.at[0, r], at_lo(r))

    def up_copy(k, r):
        src, dev = k - 1, at_link(1)
        if k == 1 and r == 0:
            src = jnp.where(last, RING, 0)
            dev = at_seq(jnp.where(last, -(RING - 1) * LO, LO))
        return copy(kv.at[src, lo_of[r]], kv.at[k, lo_of[r]], kv_send.at[k, r], kv_recv.at[k, r], dev)

    def down_copy(k, r):
        src, dev = (0, at_link(RING)) if k == RING else (k + 1, at_link(-1))
        return copy(kv.at[src, lo_of[r]], kv.at[k, lo_of[r]], kv_send.at[k, r], kv_recv.at[k, r], dev)

    def og_copy(d):
        return copy(og.at[n], og.at[n], og_send.at[d], og_recv.at[d], at_hi(d))

    def sib_copy(d):
        m = lax.rem(hi + N_HI - d, N_HI) * 2 + core
        return copy(og.at[m], og.at[m], osib_send.at[d], osib_recv.at[d], sibling)

    loads[0].wait()
    loads[1].wait()
    go_if(inner, up_copy(1, 0))
    go(down_copy(RING, 0))
    for r in (1, 2):
        go(z_copy(r))
    loads[2].wait()
    for d in (1, 2, 3):
        go_if(hi + d >= N_HI, og_copy(d))
    go(sib_copy(0))

    loads[3].wait()
    qt[...] = jnp.concatenate(
        [q_in[:, i * HD:(i + 1) * HD].astype(F32).T for i in range(GROUP)], axis=1
    ).astype(BF16)
    lane = lax.broadcasted_iota(jnp.int32, (1, WIDTH), 1)
    pos = s * TOK + lax.rem(lane, TOK)
    begin = jnp.zeros_like(pos)
    end = jnp.int32(0)
    for i in range(8):
        end = end + clip_ref[i]
        begin = jnp.where(pos >= end, end, begin)

    def scores(k):
        sc = mm(kv[k, :, 0].reshape(BUNDLE, HD), qt[...])
        row = (link - k) * BUNDLE + lax.broadcasted_iota(jnp.int32, (BUNDLE, WIDTH), 0)
        ok = row >= begin
        if k == 0:
            ok = ok & (row <= pos)
        sc = jnp.where(ok, sc, MASKED)
        s_buf[k] = sc
        top = jnp.max(sc.reshape(BUNDLE // 8, 8, WIDTH), axis=0)
        mx[...] = top if k == 0 else jnp.maximum(mx[...], top)
        for i in range(LO):
            cols = slice(k * BUNDLE + i * TOK, k * BUNDLE + (i + 1) * TOK)
            kt[:, cols] = kv[k, i, 0].T
            vt[:, cols] = kv[k, i, 1].T

    def down_step(k, r):
        down_copy(k, r).wait_recv()
        if k > (4 if r == 0 else 5):
            go(down_copy(k - 1, r))
        if k == RING and r == 0:
            go_if(last, up_copy(1, 0))

    def up_step(k, r):
        up_copy(k, r).wait_recv()
        if k < (3 if r == 0 else 4):
            go(up_copy(k + 1, r))

    def og_up(d):
        @pl.when(hi + d < N_HI)
        def _():
            pl.semaphore_wait(ready.at[d], 1)
            og_copy(d).start()

    down_step(8, 0)
    for r in (1, 2):
        z_copy(r).wait_recv()
        go(up_copy(1, r))
        go(down_copy(RING, r))
    up_step(1, 0)
    sent.append(up_copy(1, 0))
    scores(0)
    down_step(7, 0)
    up_step(2, 0)
    for r in (1, 2):
        down_step(8, r)
        up_step(1, r)
    og_up(1)
    down_step(6, 0)
    scores(8)
    scores(1)
    up_step(3, 0)
    for r in (1, 2):
        down_step(7, r)
        up_step(2, r)
    down_step(5, 0)
    og_up(2)
    og_up(3)
    scores(7)
    scores(2)
    for r in (1, 2):
        down_step(6, r)
        up_step(3, r)
    down_step(4, 0)
    scores(6)
    scores(3)
    for r in (1, 2):
        down_step(5, r)
        up_step(4, r)
    scores(5)
    scores(4)

    top = jnp.max(mx[...], axis=0, keepdims=True) * EXP2_SCALE
    total = jnp.zeros((8, WIDTH), F32)
    for k in range(RING + 1):
        p = jnp.exp2(s_buf[k] * EXP2_SCALE - top)
        total = total + jnp.sum(p.reshape(BUNDLE // 8, 8, WIDTH), axis=0)
        p_buf[k * BUNDLE:(k + 1) * BUNDLE, :] = p.astype(BF16)
    inv = 1.0 / jnp.sum(total, axis=0, keepdims=True)
    out_t = (mm(vt[...], p_buf[...]) * inv).astype(BF16).astype(F32)
    attended = jnp.concatenate([out_t[:, i * HD:(i + 1) * HD].T for i in range(GROUP)], axis=1).astype(BF16)
    att_ref[...] = attended

    def store(i, src, dst):
        c = pltpu.make_async_copy(src, dst, out_sem.at[i])
        c.start()
        return c

    stores = [store(0, att_ref, att_hbm)]

    for d in (3, 2, 1):
        og_copy(d).wait_recv()
        go(sib_copy(d))
    loads[4].wait()
    for d in (0, 3, 2, 1):
        sib_copy(d).wait_recv()
    dh = mm_t(w[:, 0:WIDTH], og[0])
    for m in range(1, N_HEAD):
        dh = dh + mm_t(w[:, m * WIDTH:(m + 1) * WIDTH], og[m])
    d_t = jnp.concatenate([dh[i * HD:(i + 1) * HD, :] for i in range(GROUP)], axis=1).astype(BF16)
    dot[...] = d_t
    d_t = d_t.astype(F32)
    delta = jnp.sum(d_t * out_t, axis=0, keepdims=True)
    dos[...] = blocks_t(d_t * inv).astype(BF16)
    qs[...] = blocks_t(qt[...].astype(F32) * (inv * SCALE)).astype(BF16)

    def backward(k):
        rows = slice(k * BUNDLE, (k + 1) * BUNDLE)
        p = p_buf[rows, :]
        dp = mm(kv[k, :, 1].reshape(BUNDLE, HD), dot[...])
        ds = (p.astype(F32) * (dp - delta)).astype(BF16)
        dv = mm(p, dos[...])
        dk = mm(ds, qs[...])
        for i in range(LO):
            acc[k, i, 0] = dk[i * TOK:(i + 1) * TOK, :]
            acc[k, i, 1] = dv[i * TOK:(i + 1) * TOK, :]
        p_buf[rows, :] = ds

    back = [lax.rem(z + r, LO) for r in range(LO)]
    order = (1, 2, 0)

    def up_back(k, r):
        dev = at_link(-1)
        if k == 1 and r == 1:
            dev = at_seq(jnp.where(y == 0, (RING - 1) * LO, -LO))
        return copy(stage.at[k, back[r]], up_in.at[k - 1, back[r]], up_send.at[k - 1, r], up_recv.at[k - 1, r], dev)

    def down_back(k, r):
        dev = at_link(-RING) if k == RING else at_link(1)
        src = stage.at[9 if k == 4 else k, back[r]]
        return copy(src, down_in.at[k - 4, back[r]], down_send.at[k - 4, r], down_recv.at[k - 4, r], dev)

    def mine(k, r):
        return acc[k, back[r]]

    def send_up(k, r):
        total = mine(k, r)
        if k < (3 if r == 1 else 4):
            up_back(k + 1, r).wait_recv()
            total = total + up_in[k, back[r]].astype(F32)
        stage[k, back[r]] = total.astype(BF16)
        go(up_back(k, r))

    def send_down(k, r):
        total = mine(k, r)
        if k > (4 if r == 1 else 5):
            down_back(k - 1, r).wait_recv()
            total = total + down_in[k - 5, back[r]].astype(F32)
        if k == RING and r == 1:

            @pl.when(last)
            def _():
                up_back(1, 1).wait_recv()
                stage[RING, back[1]] = (total + up_in[0, back[1]].astype(F32)).astype(BF16)

            @pl.when(inner)
            def _():
                stage[RING, back[1]] = total.astype(BF16)
        else:
            stage[9 if k == 4 else k, back[r]] = total.astype(BF16)
        go(down_back(k, r))

    backward(4)
    send_down(4, 1)
    send_up(4, 2)
    send_up(4, 0)
    backward(5)
    send_down(5, 2)
    send_down(5, 0)
    backward(3)
    send_up(3, 1)

    def part_copy(d):
        m = lax.rem(hi + d, N_HI) * 2 + 1 - core
        return copy(part.at[m], psib.at[d], part_send.at[d], part_recv.at[d], sibling)

    def far_copy(d):
        return copy(pmine.at[d], pfar.at[d], pfar_send.at[d], pfar_recv.at[d], at_hi(d))

    for m in range(N_HEAD):
        part[m] = mm(attended, w[:, m * WIDTH:(m + 1) * WIDTH]).astype(BF16)
    for d in (1, 2, 3, 0):
        go(part_copy(d))
    backward(6)
    send_down(5, 1)
    for r in (2, 0):
        send_up(3, r)
        send_down(6, r)
    send_down(6, 1)

    for d in (1, 2, 3, 0):
        part_copy(d).wait_recv()
        m = lax.rem(hi + d, N_HI) * 2 + core
        both = part[m].astype(F32) + psib[d].astype(F32)
        pmine[d] = both.astype(BF16)
        if d:
            go(far_copy(d))

    backward(2)
    backward(7)
    send_up(2, 1)
    for r in (2, 0):
        send_up(2, r)
        send_down(7, r)
    send_down(7, 1)
    backward(1)
    backward(8)
    send_up(1, 1)
    for r in (2, 0):
        send_up(1, r)
        send_down(8, r)
    send_down(8, 1)
    backward(0)

    def z_back(r):
        return copy(zs.at[back[r]], zr.at[r - 1], z_send.at[r - 1], z_recv.at[r - 1], at_lo(r))

    def final(r):
        total = mine(0, r)
        if r == 1:

            @pl.when(inner)
            def _():
                up_back(1, 1).wait_recv()
                acc[0, back[1]] = total + up_in[0, back[1]].astype(F32)

            total = mine(0, r)
        else:
            up_back(1, r).wait_recv()
            total = total + up_in[0, back[r]].astype(F32)
        down_back(8, r).wait_recv()
        total = total + down_in[4, back[r]].astype(F32)
        if r:
            zs[back[r]] = total.astype(BF16)
            go(z_back(r))
        return total

    final(2)
    own = final(0)
    final(1)

    dq_t = mm(kt[...], p_buf[...]) * (inv * SCALE)
    dq_ref[...] = jnp.concatenate([dq_t[:, i * HD:(i + 1) * HD].T for i in range(GROUP)], axis=1).astype(BF16)
    stores.append(store(1, dq_ref, dq_hbm))

    for d in (1, 2, 3):
        far_copy(d).wait_recv()
    mixed_ref[...] = (
        pmine[0].astype(F32) + pfar[1].astype(F32) + pfar[2].astype(F32) + pfar[3].astype(F32)
    ).astype(BF16)
    stores.append(store(2, mixed_ref, mixed_hbm))

    for r in (1, 2):
        z_back(r).wait_recv()
    own = own + zr[0].astype(F32) + zr[1].astype(F32)
    dk_ref[...] = own[0].astype(BF16)
    dv_ref[...] = own[1].astype(BF16)
    stores.append(store(3, dk_ref, dk_hbm))
    stores.append(store(4, dv_ref, dv_hbm))

    for d in (1, 2, 3):
        sent.append(og_copy(d))
    for c in sent:
        c.wait_send()
    for c in stores:
        c.wait()


def finish(*refs):
    sources, targets, sem = refs[:5], refs[5:10], refs[10]
    copies = [pltpu.make_async_copy(a, b, sem.at[i]) for i, (a, b) in enumerate(zip(sources, targets))]
    for c in copies:
        c.start()
    for c in copies:
        c.wait()


def shards(query_heads, key_heads, value_heads, out_weight, out_grad, clip_lengths):
    dma = pltpu.SemaphoreType.DMA
    vmem = pltpu.VMEM
    keys = (RING + 1) * BUNDLE
    hbm = pl.BlockSpec(memory_space=pl.ANY)
    block = jax.ShapeDtypeStruct((TOK, WIDTH), BF16)
    small = jax.ShapeDtypeStruct((TOK, HD), BF16)
    shapes = (block, block, block, small, small)
    piece = (2, TOK, HD)
    results = pl.pallas_call(
        kernel,
        out_shape=shapes,
        in_specs=[pl.BlockSpec(memory_space=pltpu.SMEM)] + [hbm] * 5,
        out_specs=[hbm] * 5,
        scratch_shapes=[
            vmem((TOK, WIDTH), BF16),
            vmem((RING + 1, LO) + piece, BF16),
            vmem((N_HEAD, TOK, WIDTH), BF16),
            vmem((WIDTH, N_HEAD * WIDTH), BF16),
            vmem((HD, WIDTH), BF16),
            vmem((WIDTH, HD), BF16),
            vmem((HD, WIDTH), BF16),
            vmem((WIDTH, HD), BF16),
            vmem((RING + 1, BUNDLE, WIDTH), F32),
            vmem((keys, WIDTH), BF16),
            vmem((HD, keys), BF16),
            vmem((HD, keys), BF16),
            vmem((8, WIDTH), F32),
            vmem((RING + 1, LO) + piece, F32),
            vmem((N_HEAD, TOK, WIDTH), BF16),
            vmem((N_HI, TOK, WIDTH), BF16),
            vmem((N_HI, TOK, WIDTH), BF16),
            vmem((N_HI, TOK, WIDTH), BF16),
            vmem((4, LO) + piece, BF16),
            vmem((5, LO) + piece, BF16),
            vmem((RING + 2, LO) + piece, BF16),
            vmem((LO,) + piece, BF16),
            vmem((LO - 1,) + piece, BF16),
            vmem((TOK, WIDTH), BF16), vmem((TOK, WIDTH), BF16), vmem((TOK, WIDTH), BF16),
            vmem((TOK, HD), BF16), vmem((TOK, HD), BF16),
            dma((5,)), dma((5,)), pltpu.SemaphoreType.REGULAR((N_HI,)),
            dma((RING + 1, LO)), dma((RING + 1, LO)),
            dma((N_HI,)), dma((N_HI,)), dma((N_HI,)), dma((N_HI,)),
            dma((N_HI,)), dma((N_HI,)), dma((N_HI,)), dma((N_HI,)),
            dma((4, LO)), dma((4, LO)), dma((5, LO)), dma((5, LO)),
            dma((LO - 1,)), dma((LO - 1,)),
        ],
        compiler_params=pltpu.CompilerParams(
            collective_id=0, has_side_effects=True, vmem_limit_bytes=60 * 1024 * 1024
        ),
        cost_estimate=pl.CostEstimate(flops=3_000_000_000, bytes_accessed=4_000_000, transcendentals=1_400_000),
    )(clip_lengths, query_heads, key_heads, value_heads, out_grad, out_weight)
    return pl.pallas_call(
        finish,
        out_shape=shapes,
        in_specs=[hbm] * 5,
        out_specs=[hbm] * 5,
        scratch_shapes=[dma((5,))],
    )(*results)


def solution(mesh):
    wide = P("seq", "head")
    return jax.shard_map(
        shards,
        mesh=mesh,
        in_specs=(wide, wide, wide, P("head", None), wide, P()),
        out_specs=(wide,) * 5,
        check_vma=False,
    )
```

time: 90.2 us -> 91.9 us (1.019)
  the two profiles are of different devices: /device:TPU:198 before, /device:TPU:1 now
where the time goes in v2:
time: 91.9 us; the launch traced here: 91.7 us
  Pallas kernels  91.1 us (99%)
    pallas_call x1, Pallas kernels, shards(): pl.pallas_call(kernel, out_shape=shapes, in_specs=[pl.BlockSpec(memory_sp...  79 us
    pallas_call x1, Pallas kernels, shards(): pl.pallas_call(finish, out_shape=shapes, in_specs=[hbm] * 5, out_specs=[h...  12.1 us

profile of v2, /device:TPU:1, one launch (start us, length us, event | category | flops | bytes accessed | tf_op | source)
XLA Modules:
  0.0 91.7 jit_solution(3520499760171443342)
XLA Ops:
  0.6 79.0 %shard_map.101 = (bf16[128,384]{1,0:T(8,128)(2,1)}, bf16[128,384]{1,0:T(8,128)(2,1)}, bf16[128,384]{1,0:T(8,128)(2,1)}, bf16[128,128]{1,0:T(8,128)(2,1)}, bf16[128,128]{1,0:T(8,128)(2,1)}) custom-call(s32[8]{0:T(128)} %clip_ref.1, bf16[128,384]{1,0:T(8,128)(2,1)} %q_hbm.1, bf16[128,128]{1,0:T(8,128)(2,1)} %k_hbm.1, bf16[128,128]{1,0:T(8,128)(2,1)} %v_hbm.1, ...), custom_call_target="tpu_custom_call" | custom-call | flops 3000000000 | bytes 4000000 | tf_op jit(solution)/shard_map/pallas_call | solution.py:448
  79.7 12.1 %shard_map.102 = (bf16[128,384]{1,0:T(8,128)(2,1)}, bf16[128,384]{1,0:T(8,128)(2,1)}, bf16[128,384]{1,0:T(8,128)(2,1)}, bf16[128,128]{1,0:T(8,128)(2,1)}, bf16[128,128]{1,0:T(8,128)(2,1)}) custom-call(bf16[128,384]{1,0:T(8,128)(2,1)} %get-tuple-element.10.refs_0_, bf16[128,384]{1,0:T(8,128)(2,1)} %get-tuple-element.11.refs_1_, ...), custom_call_target="tpu_custom_call" | custom-call | tf_op jit(solution)/shard_map/pallas_call | solution.py:491

commit v3 on v2

v3 whole, which is shorter than its diff:
```python
import math

import jax
import jax.numpy as jnp
from jax import lax
from jax.experimental import pallas as pl
from jax.experimental.pallas import tpu as pltpu
from jax.sharding import PartitionSpec as P

HD = 128
GROUP = 3
TOK = 128
LO = 3
LINKS = 32
RING = 8
N_SEQ = LO * LINKS
N_HEAD = 8
N_HI = 4
WIDTH = GROUP * HD
BUNDLE = LO * TOK
SCALE = 1.0 / math.sqrt(HD)
EXP2_SCALE = SCALE * math.log2(math.e)
MASKED = -1e30
MESH = pl.DeviceIdType.MESH
F32 = jnp.float32
BF16 = jnp.bfloat16


def mm(a, b):
    return jnp.dot(a, b, preferred_element_type=F32)


def mm_t(a, b):
    return lax.dot_general(a, b, (((1,), (1,)), ((), ())), preferred_element_type=F32)


def blocks_t(x):
    if x.shape[0] == HD:
        return jnp.concatenate([x[:, i * HD:(i + 1) * HD].T for i in range(GROUP)], axis=0)
    return jnp.concatenate([x[i * HD:(i + 1) * HD, :].T for i in range(GROUP)], axis=1)


def kernel(
    clip_ref, q_hbm, k_hbm, v_hbm, og_hbm, w_hbm,
    mixed_hbm, att_hbm, dq_hbm, dk_hbm, dv_hbm,
    q_in, kv, og, w, qt, qs, dot, dos, s_buf, p_buf, kt, vt, mx, acc,
    part, psib, pmine, pfar, come, mate, stage,
    mixed_ref, att_ref, dq_ref, dk_ref, dv_ref,
    in_sem, out_sem, ready,
    kv_send, kv_recv, lo_send, lo_recv, og_send, og_recv, osib_send, osib_recv,
    part_send, part_recv, pfar_send, pfar_recv,
    up_send, up_recv, z_send, z_recv,
):
    s = lax.axis_index("seq")
    n = lax.axis_index("head")
    link, z = lax.div(s, LO), lax.rem(s, LO)
    hi, core = lax.div(n, 2), lax.rem(n, 2)
    y = lax.rem(link, RING)
    first, last = y == 0, y == RING - 1
    not_first, not_last = y > 0, y < RING - 1

    def at_seq(step):
        return (lax.rem(s + step + N_SEQ, N_SEQ), n)

    def at_link(step):
        return at_seq(step * LO)

    def at_lo(r):
        return (link * LO + lax.rem(z + r, LO), n)

    def at_hi(d):
        return (s, lax.rem(hi + d, N_HI) * 2 + core)

    sibling = (s, hi * 2 + 1 - core)
    lo_of = [lax.rem(z + LO - r, LO) for r in range(LO)]

    def copy(src, dst, ssem, rsem, dev):
        return pltpu.make_async_remote_copy(
            src_ref=src, dst_ref=dst, send_sem=ssem, recv_sem=rsem, device_id=dev, device_id_type=MESH
        )

    sent = []

    def go(c):
        c.start()
        sent.append((None, c))

    def go_if(cond, c):
        pl.when(cond)(c.start)
        sent.append((cond, c))

    def load(i, src, dst):
        c = pltpu.make_async_copy(src, dst, in_sem.at[i])
        c.start()
        return c

    loads = [
        load(0, k_hbm, kv.at[0, z, 0]), load(1, v_hbm, kv.at[0, z, 1]),
        load(2, og_hbm, og.at[n]), load(3, q_hbm, q_in), load(4, w_hbm, w),
    ]

    barrier = pltpu.get_barrier_semaphore()
    near = [at_link(step * sign) for step in (1, 2, 6, RING) for sign in (1, -1)]
    near += [at_lo(1), at_lo(2), sibling]
    for dev in near:
        pl.semaphore_signal(barrier, inc=1, device_id=dev, device_id_type=MESH)

    def greet(cond, dev, sem):
        @pl.when(cond)
        def _():
            pl.semaphore_signal(sem, inc=1, device_id=dev, device_id_type=MESH)

    for d in (1, 2, 3):
        greet(hi + d < N_HI, at_hi(d), barrier)
    wrap = (RING - 1) * LO
    greet(first, at_seq(wrap), barrier)
    greet(last, at_seq(-wrap), barrier)
    pl.semaphore_wait(barrier, len(near) + hi + jnp.where(first | last, 1, 0))
    for d in (1, 2, 3):
        greet(hi + d >= N_HI, at_hi(d), ready.at[N_HI - d])

    def way(k, r):
        return {1: 1, 2: 1 if r else 2, 3: 1, 4: -2, 5: -1, 6: -1 if r else 6, 7: -1, RING: RING}[k]

    def move(k, r):
        step = way(k, r)
        return copy(
            kv.at[k - step, lo_of[r]], kv.at[k, lo_of[r]], kv_send.at[k, r], kv_recv.at[k, r], at_link(step)
        )

    def wrapped():
        return copy(kv.at[RING, z], kv.at[1, z], kv_send.at[1, 0], kv_recv.at[1, 0], at_seq(-wrap))

    def shared(r):
        return copy(kv.at[RING, z], kv.at[RING, z], kv_send.at[RING, r], kv_recv.at[RING, r], at_lo(r))

    def spread(k, r):
        return copy(kv.at[k, z], kv.at[k, z], lo_send.at[k, r], lo_recv.at[k, r], at_lo(r))

    def og_copy(d):
        return copy(og.at[n], og.at[n], og_send.at[d], og_recv.at[d], at_hi(d))

    def sib_copy(d):
        m = lax.rem(hi + N_HI - d, N_HI) * 2 + core
        return copy(og.at[m], og.at[m], osib_send.at[d], osib_recv.at[d], sibling)

    loads[0].wait()
    loads[1].wait()
    go(move(RING, 0))
    go(move(6, 0))
    go(move(2, 0))
    go_if(not_last, move(1, 0))
    for r in (1, 2):
        go(spread(0, r))
    loads[3].wait()
    qt[...] = jnp.concatenate(
        [q_in[:, i * HD:(i + 1) * HD].astype(F32).T for i in range(GROUP)], axis=1
    ).astype(BF16)
    lane = lax.broadcasted_iota(jnp.int32, (1, WIDTH), 1)
    pos = s * TOK + lax.rem(lane, TOK)
    begin = jnp.zeros_like(pos)
    end = jnp.int32(0)
    for i in range(8):
        end = end + clip_ref[i]
        begin = jnp.where(pos >= end, end, begin)

    def scores(k):
        sc = mm(kv[k, :, 0].reshape(BUNDLE, HD), qt[...])
        row = (link - k) * BUNDLE + lax.broadcasted_iota(jnp.int32, (BUNDLE, WIDTH), 0)
        ok = row >= begin
        if k == 0:
            ok = ok & (row <= pos)
        sc = jnp.where(ok, sc, MASKED)
        s_buf[k] = sc
        top = jnp.max(sc.reshape(BUNDLE // 8, 8, WIDTH), axis=0)
        mx[...] = top if k == 0 else jnp.maximum(mx[...], top)
        for i in range(LO):
            cols = slice(k * BUNDLE + i * TOK, k * BUNDLE + (i + 1) * TOK)
            kt[:, cols] = kv[k, i, 0].T
            vt[:, cols] = kv[k, i, 1].T

    def og_up(d):
        @pl.when(hi + d < N_HI)
        def _():
            pl.semaphore_wait(ready.at[d], 1)
            og_copy(d).start()

    def got(k, r, *then):
        move(k, r).wait_recv()
        for c in then:
            go(c)

    got(6, 0, move(5, 0), move(4, 0))
    got(2, 0, move(3, 0))
    got(RING, 0, move(7, 0))
    go_if(last, wrapped())
    for r in (1, 2):
        go_if(first, shared(r))
    for r in (1, 2):
        spread(0, r).wait_recv()
        go(move(1, r))
        go_if(not_first, move(RING, r))
    loads[2].wait()
    for d in (1, 2, 3):
        go_if(hi + d >= N_HI, og_copy(d))
    go(sib_copy(0))
    got(1, 0)
    scores(0)
    got(5, 0, spread(5, 1), spread(5, 2))
    for r in (1, 2):
        got(RING, r, move(7, r))
        got(1, r, move(2, r))
    got(4, 0, spread(4, 1), spread(4, 2))
    got(7, 0)
    got(3, 0)
    og_up(1)
    scores(1)
    scores(RING)
    for r in (1, 2):
        got(7, r, move(6, r))
        got(2, r, move(3, r))
    scores(2)
    scores(7)
    for k in (5, 4):
        for r in (1, 2):
            spread(k, r).wait_recv()
        scores(k)
    for k in (6, 3):
        for r in (1, 2):
            got(k, r)
        scores(k)
    og_up(2)
    og_up(3)

    top = jnp.max(mx[...], axis=0, keepdims=True) * EXP2_SCALE
    total = jnp.zeros((8, WIDTH), F32)
    for k in range(RING + 1):
        p = jnp.exp2(s_buf[k] * EXP2_SCALE - top)
        total = total + jnp.sum(p.reshape(BUNDLE // 8, 8, WIDTH), axis=0)
        p_buf[k * BUNDLE:(k + 1) * BUNDLE, :] = p.astype(BF16)
    inv = 1.0 / jnp.sum(total, axis=0, keepdims=True)
    out_t = (mm(vt[...], p_buf[...]) * inv).astype(BF16).astype(F32)
    attended = jnp.concatenate([out_t[:, i * HD:(i + 1) * HD].T for i in range(GROUP)], axis=1).astype(BF16)
    att_ref[...] = attended

    def store(i, src, dst):
        c = pltpu.make_async_copy(src, dst, out_sem.at[i])
        c.start()
        return c

    stores = [store(0, att_ref, att_hbm)]

    def part_copy(d):
        m = lax.rem(hi + d, N_HI) * 2 + 1 - core
        return copy(part.at[m], psib.at[d], part_send.at[d], part_recv.at[d], sibling)

    def far_copy(d):
        return copy(pmine.at[d], pfar.at[d], pfar_send.at[d], pfar_recv.at[d], at_hi(d))

    loads[4].wait()
    for d in (1, 2, 3, 0):
        m = lax.rem(hi + d, N_HI) * 2 + 1 - core
        part[m] = mm(attended, w[:, pl.ds(pl.multiple_of(m * WIDTH, HD), WIDTH)]).astype(BF16)
        go(part_copy(d))
    for d in (1, 2, 3, 0):
        m = lax.rem(hi + d, N_HI) * 2 + core
        part[m] = mm(attended, w[:, pl.ds(pl.multiple_of(m * WIDTH, HD), WIDTH)]).astype(BF16)
    for d in (1, 2, 3, 0):
        part_copy(d).wait_recv()
        m = lax.rem(hi + d, N_HI) * 2 + core
        both = part[m].astype(F32) + psib[d].astype(F32)
        pmine[d] = both.astype(BF16)
        if d:
            go(far_copy(d))

    for d in (3, 2, 1):
        og_copy(d).wait_recv()
        go(sib_copy(d))
    for d in (0, 3, 2, 1):
        sib_copy(d).wait_recv()
    dh = mm_t(w[:, 0:WIDTH], og[0])
    for m in range(1, N_HEAD):
        dh = dh + mm_t(w[:, m * WIDTH:(m + 1) * WIDTH], og[m])
    d_t = jnp.concatenate([dh[i * HD:(i + 1) * HD, :] for i in range(GROUP)], axis=1).astype(BF16)
    dot[...] = d_t
    d_t = d_t.astype(F32)
    delta = jnp.sum(d_t * out_t, axis=0, keepdims=True)
    dos[...] = blocks_t(d_t * inv).astype(BF16)
    qs[...] = blocks_t(qt[...].astype(F32) * (inv * SCALE)).astype(BF16)

    def backward(k):
        rows = slice(k * BUNDLE, (k + 1) * BUNDLE)
        p = p_buf[rows, :]
        dp = mm(kv[k, :, 1].reshape(BUNDLE, HD), dot[...])
        ds = (p.astype(F32) * (dp - delta)).astype(BF16)
        dv = mm(p, dos[...])
        dk = mm(ds, qs[...])
        for i in range(LO):
            acc[k, i, 0] = dk[i * TOK:(i + 1) * TOK, :]
            acc[k, i, 1] = dv[i * TOK:(i + 1) * TOK, :]
        p_buf[rows, :] = ds

    back = [lax.rem(z + r, LO) for r in range(LO)]

    def give(k, r):
        step = way(k, r)
        return copy(stage.at[k, back[r]], come.at[k, back[r]], up_send.at[k, r], up_recv.at[k, r], at_link(-step))

    def give_wrapped():
        return copy(stage.at[1, z], come.at[1, z], up_send.at[1, 0], up_recv.at[1, 0], at_seq(wrap))

    def gather(k, r):
        return copy(stage.at[k, back[r]], mate.at[k, r], z_send.at[k, r], z_recv.at[k, r], at_lo(r))

    def fill(k, r, *terms):
        total = acc[k, back[r]]
        for t in terms:
            total = total + t.astype(F32)
        stage[k, back[r]] = total.astype(BF16)

    def send(c, k, r, *terms):
        fill(k, r, *terms)
        go(c)

    def came(k, r):
        give(k, r).wait_recv()
        return come[k, back[r]]

    def mates(k):
        for r in (1, 2):
            gather(k, r).wait_recv()
        return mate[k, 1].astype(F32) + mate[k, 2].astype(F32)

    backward(3)
    for r in (1, 2, 0):
        send(give(3, r), 3, r)
    backward(6)
    for r in (1, 2):
        send(give(6, r), 6, r)
    for k in (4, 5):
        backward(k)
        for r in (1, 2):
            send(gather(k, r), k, r)
    backward(7)
    send(give(7, 0), 7, 0)
    backward(2)

    for r in (1, 2):
        send(give(2, r), 2, r, came(3, r))
        send(give(7, r), 7, r, came(6, r))
    send(give(4, 0), 4, 0, mates(4))
    send(give(5, 0), 5, 0, mates(5))
    send(give(2, 0), 2, 0, came(3, 0))

    backward(RING)
    backward(1)
    fill(1, 0)
    go_if(not_first, give(1, 0))
    go_if(first, give_wrapped())
    for r in (1, 2):
        send(give(1, r), 1, r, came(2, r))
        fill(RING, r, came(7, r))
        go_if(not_first, give(RING, r))
        go_if(first, gather(RING, r))
    send(give(6, 0), 6, 0, came(4, 0), came(5, 0))

    @pl.when(first)
    def _():
        fill(RING, 0, came(7, 0), mates(RING))

    @pl.when(last)
    def _():
        fill(RING, 0, came(7, 0), came(1, 0))

    @pl.when(not_first & not_last)
    def _():
        fill(RING, 0, came(7, 0))

    go(give(RING, 0))
    backward(0)
    for r in (1, 2):

        @pl.when(first)
        def _():
            fill(0, r, came(1, r))

        @pl.when(not_first)
        def _():
            fill(0, r, came(1, r), came(RING, r))

        go(gather(0, r))

    dq_t = mm(kt[...], p_buf[...]) * (inv * SCALE)
    dq_ref[...] = jnp.concatenate([dq_t[:, i * HD:(i + 1) * HD].T for i in range(GROUP)], axis=1).astype(BF16)
    stores.append(store(1, dq_ref, dq_hbm))

    for d in (1, 2, 3):
        far_copy(d).wait_recv()
    mixed_ref[...] = (
        pmine[0].astype(F32) + pfar[1].astype(F32) + pfar[2].astype(F32) + pfar[3].astype(F32)
    ).astype(BF16)
    stores.append(store(2, mixed_ref, mixed_hbm))

    @pl.when(not_last)
    def _():
        acc[0, z] = acc[0, z] + came(1, 0).astype(F32)

    own = acc[0, z]
    for k in (2, 6, RING):
        own = own + came(k, 0).astype(F32)
    own = own + mates(0)
    dk_ref[...] = own[0].astype(BF16)
    dv_ref[...] = own[1].astype(BF16)
    stores.append(store(3, dk_ref, dk_hbm))
    stores.append(store(4, dv_ref, dv_hbm))

    for d in (1, 2, 3):
        sent.append((hi + d < N_HI, og_copy(d)))
    for cond, c in sent:
        c.wait_send() if cond is None else pl.when(cond)(c.wait_send)
    for c in stores:
        c.wait()


def finish(*refs):
    for source, target in zip(refs[:5], refs[5:]):
        target[...] = source[...]


def shards(query_heads, key_heads, value_heads, out_weight, out_grad, clip_lengths):
    dma = pltpu.SemaphoreType.DMA
    vmem = pltpu.VMEM
    keys = (RING + 1) * BUNDLE
    hbm = pl.BlockSpec(memory_space=pl.ANY)
    block = jax.ShapeDtypeStruct((TOK, WIDTH), BF16)
    small = jax.ShapeDtypeStruct((TOK, HD), BF16)
    shapes = (block, block, block, small, small)
    piece = (2, TOK, HD)
    results = pl.pallas_call(
        kernel,
        out_shape=shapes,
        in_specs=[pl.BlockSpec(memory_space=pltpu.SMEM)] + [hbm] * 5,
        out_specs=[hbm] * 5,
        scratch_shapes=[
            vmem((TOK, WIDTH), BF16),
            vmem((RING + 1, LO) + piece, BF16),
            vmem((N_HEAD, TOK, WIDTH), BF16),
            vmem((WIDTH, N_HEAD * WIDTH), BF16),
            vmem((HD, WIDTH), BF16),
            vmem((WIDTH, HD), BF16),
            vmem((HD, WIDTH), BF16),
            vmem((WIDTH, HD), BF16),
            vmem((RING + 1, BUNDLE, WIDTH), F32),
            vmem((keys, WIDTH), BF16),
            vmem((HD, keys), BF16),
            vmem((HD, keys), BF16),
            vmem((8, WIDTH), F32),
            vmem((RING + 1, LO) + piece, F32),
            vmem((N_HEAD, TOK, WIDTH), BF16),
            vmem((N_HI, TOK, WIDTH), BF16),
            vmem((N_HI, TOK, WIDTH), BF16),
            vmem((N_HI, TOK, WIDTH), BF16),
            vmem((RING + 1, LO) + piece, BF16),
            vmem((RING + 1, LO) + piece, BF16),
            vmem((RING + 1, LO) + piece, BF16),
            vmem((TOK, WIDTH), BF16), vmem((TOK, WIDTH), BF16), vmem((TOK, WIDTH), BF16),
            vmem((TOK, HD), BF16), vmem((TOK, HD), BF16),
            dma((5,)), dma((5,)), pltpu.SemaphoreType.REGULAR((N_HI,)),
            dma((RING + 1, LO)), dma((RING + 1, LO)), dma((RING + 1, LO)), dma((RING + 1, LO)),
            dma((N_HI,)), dma((N_HI,)), dma((N_HI,)), dma((N_HI,)),
            dma((N_HI,)), dma((N_HI,)), dma((N_HI,)), dma((N_HI,)),
            dma((RING + 1, LO)), dma((RING + 1, LO)), dma((RING + 1, LO)), dma((RING + 1, LO)),
        ],
        compiler_params=pltpu.CompilerParams(
            collective_id=0, has_side_effects=True, vmem_limit_bytes=60 * 1024 * 1024
        ),
        cost_estimate=pl.CostEstimate(flops=3_000_000_000, bytes_accessed=4_000_000, transcendentals=1_400_000),
    )(clip_lengths, query_heads, key_heads, value_heads, out_grad, out_weight)
    return pl.pallas_call(
        finish,
        out_shape=shapes,
        in_specs=[pl.BlockSpec(memory_space=pltpu.VMEM)] * 5,
        out_specs=[pl.BlockSpec(memory_space=pltpu.VMEM)] * 5,
        compiler_params=pltpu.CompilerParams(vmem_limit_bytes=60 * 1024 * 1024),
    )(*results)


def solution(mesh):
    wide = P("seq", "head")
    return jax.shard_map(
        shards,
        mesh=mesh,
        in_specs=(wide, wide, wide, P("head", None), wide, P()),
        out_specs=(wide,) * 5,
        check_vma=False,
    )
```

time: 91.9 us -> 80.6 us (0.88)
  Pallas kernels: 91.1 us -> 79.3 us
    pallas_call x1, Pallas kernels: 12.1 us -> 1.75 us  [shards(): pl.pallas_call(finish, out_shape=shapes, in_specs=[pl.BlockSpec(memory_sp...]
    pallas_call x1, Pallas kernels: 79 us -> 77.5 us  [shards(): pl.pallas_call(kernel, out_shape=shapes, in_specs=[pl.BlockSpec(memory_sp...]
where the time goes in v3:
time: 80.6 us; the launch traced here: 79.9 us
  Pallas kernels  79.3 us (98%)
    pallas_call x1, Pallas kernels, shards(): pl.pallas_call(kernel, out_shape=shapes, in_specs=[pl.BlockSpec(memory_sp...  77.5 us
    pallas_call x1, Pallas kernels, shards(): pl.pallas_call(finish, out_shape=shapes, in_specs=[pl.BlockSpec(memory_sp...  1.75 us

profile of v3, /device:TPU:1, one launch (start us, length us, event | category | flops | bytes accessed | tf_op | source)
XLA Modules:
  0.0 79.9 jit_solution(13909938266861121082)
XLA Ops:
  0.6 77.5 %shard_map.101 = (bf16[128,384]{1,0:T(8,128)(2,1)}, bf16[128,384]{1,0:T(8,128)(2,1)}, bf16[128,384]{1,0:T(8,128)(2,1)}, bf16[128,128]{1,0:T(8,128)(2,1)}, bf16[128,128]{1,0:T(8,128)(2,1)}) custom-call(s32[8]{0:T(128)} %clip_ref.1, bf16[128,384]{1,0:T(8,128)(2,1)} %q_hbm.1, bf16[128,128]{1,0:T(8,128)(2,1)} %k_hbm.1, bf16[128,128]{1,0:T(8,128)(2,1)} %v_hbm.1, ...), custom_call_target="tpu_custom_call" | custom-call | flops 3000000000 | bytes 4000000 | tf_op jit(solution)/shard_map/pallas_call | solution.py:439
  78.2 1.7 %shard_map.102 = (bf16[128,384]{1,0:T(8,128)(2,1)}, bf16[128,384]{1,0:T(8,128)(2,1)}, bf16[128,384]{1,0:T(8,128)(2,1)}, bf16[128,128]{1,0:T(8,128)(2,1)}, bf16[128,128]{1,0:T(8,128)(2,1)}) custom-call(bf16[128,384]{1,0:T(8,128)(2,1)} %get-tuple-element.10.refs_0_, bf16[128,384]{1,0:T(8,128)(2,1)} %get-tuple-element.11.refs_1_, ...), custom_call_target="tpu_custom_call" | custom-call | tf_op jit(solution)/shard_map/pallas_call | solution.py:479

commit v4 on v3

--- a/solution.py
+++ b/solution.py
@@ -120,7 +120,7 @@
         greet(hi + d >= N_HI, at_hi(d), ready.at[N_HI - d])
 
     def way(k, r):
-        return {1: 1, 2: 1 if r else 2, 3: 1, 4: -2, 5: -1, 6: -1 if r else 6, 7: -1, RING: RING}[k]
+        return {1: 1, 2: 1, 3: 1, 4: 1 if r else -1, 5: -1, 6: -1, 7: -1, RING: RING}[k]
 
     def move(k, r):
         step = way(k, r)
@@ -147,8 +147,6 @@
     loads[0].wait()
     loads[1].wait()
     go(move(RING, 0))
-    go(move(6, 0))
-    go(move(2, 0))
     go_if(not_last, move(1, 0))
     for r in (1, 2):
         go(spread(0, r))
@@ -164,6 +162,10 @@
         end = end + clip_ref[i]
         begin = jnp.where(pos >= end, end, begin)
 
+    def part_of(k):
+        at = (0, 1, 2, 3, 7, 8, 4, 5, 6)[k] * BUNDLE
+        return slice(at, at + BUNDLE)
+
     def scores(k):
         sc = mm(kv[k, :, 0].reshape(BUNDLE, HD), qt[...])
         row = (link - k) * BUNDLE + lax.broadcasted_iota(jnp.int32, (BUNDLE, WIDTH), 0)
@@ -173,14 +175,17 @@
         sc = jnp.where(ok, sc, MASKED)
         s_buf[k] = sc
         top = jnp.max(sc.reshape(BUNDLE // 8, 8, WIDTH), axis=0)
-        mx[...] = top if k == 0 else jnp.maximum(mx[...], top)
+        mx[...] = top if k in (0, 5) else jnp.maximum(mx[...], top)
+        at = part_of(k).start
         for i in range(LO):
-            cols = slice(k * BUNDLE + i * TOK, k * BUNDLE + (i + 1) * TOK)
+            cols = slice(at + i * TOK, at + (i + 1) * TOK)
             kt[:, cols] = kv[k, i, 0].T
             vt[:, cols] = kv[k, i, 1].T
 
-    def og_up(d):
-        @pl.when(hi + d < N_HI)
+    def og_up(d, early):
+        far = hi < 1 if d > 1 else hi > N_HI
+
+        @pl.when((hi + d < N_HI) & (jnp.logical_not(far) if early else far))
         def _():
             pl.semaphore_wait(ready.at[d], 1)
             og_copy(d).start()
@@ -190,8 +195,6 @@
         for c in then:
             go(c)
 
-    got(6, 0, move(5, 0), move(4, 0))
-    got(2, 0, move(3, 0))
     got(RING, 0, move(7, 0))
     go_if(last, wrapped())
     for r in (1, 2):
@@ -204,75 +207,46 @@
     for d in (1, 2, 3):
         go_if(hi + d >= N_HI, og_copy(d))
     go(sib_copy(0))
-    got(1, 0)
+    got(1, 0, move(2, 0))
+    got(7, 0, move(6, 0))
     scores(0)
-    got(5, 0, spread(5, 1), spread(5, 2))
     for r in (1, 2):
         got(RING, r, move(7, r))
         got(1, r, move(2, r))
-    got(4, 0, spread(4, 1), spread(4, 2))
-    got(7, 0)
-    got(3, 0)
-    og_up(1)
+    got(2, 0, move(3, 0))
+    got(6, 0, move(5, 0))
+    for d in (1, 2, 3):
+        og_up(d, True)
     scores(1)
     scores(RING)
     for r in (1, 2):
         got(7, r, move(6, r))
         got(2, r, move(3, r))
+    got(3, 0)
+    got(5, 0, move(4, 0))
+    for d in (2, 3):
+        og_up(d, False)
     scores(2)
     scores(7)
-    for k in (5, 4):
-        for r in (1, 2):
-            spread(k, r).wait_recv()
-        scores(k)
-    for k in (6, 3):
-        for r in (1, 2):
-            got(k, r)
-        scores(k)
-    og_up(2)
-    og_up(3)
-
+    for r in (1, 2):
+        got(6, r, move(5, r))
+        got(3, r, move(4, r))
+    scores(3)
+    scores(6)
+    def weigh(bundles, top):
+        total = jnp.zeros((8, WIDTH), F32)
+        for k in bundles:
+            p = jnp.exp2(s_buf[k] * EXP2_SCALE - top)
+            total = total + jnp.sum(p.reshape(BUNDLE // 8, 8, WIDTH), axis=0)
+            p_buf[part_of(k), :] = p.astype(BF16)
+        return jnp.sum(total, axis=0, keepdims=True)
+
+    near_part, far_part = slice(0, 7 * BUNDLE), slice(7 * BUNDLE, 9 * BUNDLE)
     top = jnp.max(mx[...], axis=0, keepdims=True) * EXP2_SCALE
-    total = jnp.zeros((8, WIDTH), F32)
-    for k in range(RING + 1):
-        p = jnp.exp2(s_buf[k] * EXP2_SCALE - top)
-        total = total + jnp.sum(p.reshape(BUNDLE // 8, 8, WIDTH), axis=0)
-        p_buf[k * BUNDLE:(k + 1) * BUNDLE, :] = p.astype(BF16)
-    inv = 1.0 / jnp.sum(total, axis=0, keepdims=True)
-    out_t = (mm(vt[...], p_buf[...]) * inv).astype(BF16).astype(F32)
-    attended = jnp.concatenate([out_t[:, i * HD:(i + 1) * HD].T for i in range(GROUP)], axis=1).astype(BF16)
-    att_ref[...] = attended
-
-    def store(i, src, dst):
-        c = pltpu.make_async_copy(src, dst, out_sem.at[i])
-        c.start()
-        return c
-
-    stores = [store(0, att_ref, att_hbm)]
-
-    def part_copy(d):
-        m = lax.rem(hi + d, N_HI) * 2 + 1 - core
-        return copy(part.at[m], psib.at[d], part_send.at[d], part_recv.at[d], sibling)
-
-    def far_copy(d):
-        return copy(pmine.at[d], pfar.at[d], pfar_send.at[d], pfar_recv.at[d], at_hi(d))
+    total = weigh((0, 1, 2, 3, 6, 7, 8), top)
+    near_out = mm(vt[:, near_part], p_buf[near_part, :])
 
     loads[4].wait()
-    for d in (1, 2, 3, 0):
-        m = lax.rem(hi + d, N_HI) * 2 + 1 - core
-        part[m] = mm(attended, w[:, pl.ds(pl.multiple_of(m * WIDTH, HD), WIDTH)]).astype(BF16)
-        go(part_copy(d))
-    for d in (1, 2, 3, 0):
-        m = lax.rem(hi + d, N_HI) * 2 + core
-        part[m] = mm(attended, w[:, pl.ds(pl.multiple_of(m * WIDTH, HD), WIDTH)]).astype(BF16)
-    for d in (1, 2, 3, 0):
-        part_copy(d).wait_recv()
-        m = lax.rem(hi + d, N_HI) * 2 + core
-        both = part[m].astype(F32) + psib[d].astype(F32)
-        pmine[d] = both.astype(BF16)
-        if d:
-            go(far_copy(d))
-
     for d in (3, 2, 1):
         og_copy(d).wait_recv()
         go(sib_copy(d))
@@ -283,18 +257,55 @@
         dh = dh + mm_t(w[:, m * WIDTH:(m + 1) * WIDTH], og[m])
     d_t = jnp.concatenate([dh[i * HD:(i + 1) * HD, :] for i in range(GROUP)], axis=1).astype(BF16)
     dot[...] = d_t
+    got(4, 0)
+    for r in (1, 2):
+        got(5, r)
+        got(4, r)
+    scores(5)
+    scores(4)
+    top_all = jnp.maximum(top, jnp.max(mx[...], axis=0, keepdims=True) * EXP2_SCALE)
+    fade = jnp.exp2(top - top_all)
+    total = total * fade + weigh((4, 5), top_all)
+    inv = 1.0 / total
+    out_t = near_out * fade + mm(vt[:, far_part], p_buf[far_part, :])
+    out_t = (out_t * inv).astype(BF16).astype(F32)
+    attended = jnp.concatenate([out_t[:, i * HD:(i + 1) * HD].T for i in range(GROUP)], axis=1).astype(BF16)
+    att_ref[...] = attended
+
+    def store(i, src, dst):
+        c = pltpu.make_async_copy(src, dst, out_sem.at[i])
+        c.start()
+        return c
+
+    stores = [store(0, att_ref, att_hbm)]
+
+    def part_copy(d):
+        m = lax.rem(hi + d, N_HI) * 2 + 1 - core
+        return copy(part.at[m], psib.at[d], part_send.at[d], part_recv.at[d], sibling)
+
+    def far_copy(d):
+        return copy(pmine.at[d], pfar.at[d], pfar_send.at[d], pfar_recv.at[d], at_hi(d))
+
+    for d in (1, 2, 3, 0):
+        m = lax.rem(hi + d, N_HI) * 2 + 1 - core
+        part[m] = mm(attended, w[:, pl.ds(pl.multiple_of(m * WIDTH, HD), WIDTH)]).astype(BF16)
+        go(part_copy(d))
+    for d in (1, 2, 3, 0):
+        m = lax.rem(hi + d, N_HI) * 2 + core
+        part[m] = mm(attended, w[:, pl.ds(pl.multiple_of(m * WIDTH, HD), WIDTH)]).astype(BF16)
     d_t = d_t.astype(F32)
     delta = jnp.sum(d_t * out_t, axis=0, keepdims=True)
-    dos[...] = blocks_t(d_t * inv).astype(BF16)
-    qs[...] = blocks_t(qt[...].astype(F32) * (inv * SCALE)).astype(BF16)
+    for i, factor in enumerate((inv * fade, inv)):
+        dos[i] = blocks_t(d_t * factor).astype(BF16)
+        qs[i] = blocks_t(qt[...].astype(F32) * (factor * SCALE)).astype(BF16)
 
     def backward(k):
-        rows = slice(k * BUNDLE, (k + 1) * BUNDLE)
+        rows, i = part_of(k), 1 if k in (4, 5) else 0
         p = p_buf[rows, :]
         dp = mm(kv[k, :, 1].reshape(BUNDLE, HD), dot[...])
         ds = (p.astype(F32) * (dp - delta)).astype(BF16)
-        dv = mm(p, dos[...])
-        dk = mm(ds, qs[...])
+        dv = mm(p, dos[i])
+        dk = mm(ds, qs[i])
         for i in range(LO):
             acc[k, i, 0] = dk[i * TOK:(i + 1) * TOK, :]
             acc[k, i, 1] = dv[i * TOK:(i + 1) * TOK, :]
@@ -331,30 +342,40 @@
             gather(k, r).wait_recv()
         return mate[k, 1].astype(F32) + mate[k, 2].astype(F32)
 
+    backward(4)
+    for r in (1, 2, 0):
+        send(give(4, r), 4, r)
+    backward(5)
+    for r in (1, 2):
+        send(give(5, r), 5, r)
+    for d in (1, 2, 3, 0):
+        part_copy(d).wait_recv()
+        m = lax.rem(hi + d, N_HI) * 2 + core
+        both = part[m].astype(F32) + psib[d].astype(F32)
+        pmine[d] = both.astype(BF16)
+        if d:
+            go(far_copy(d))
+
     backward(3)
-    for r in (1, 2, 0):
-        send(give(3, r), 3, r)
     backward(6)
-    for r in (1, 2):
-        send(give(6, r), 6, r)
-    for k in (4, 5):
-        backward(k)
-        for r in (1, 2):
-            send(gather(k, r), k, r)
+
+    for r in (1, 2):
+        send(give(3, r), 3, r, came(4, r))
+        send(give(6, r), 6, r, came(5, r))
+    send(give(3, 0), 3, 0)
+    send(give(5, 0), 5, 0, came(4, 0))
     backward(7)
-    send(give(7, 0), 7, 0)
     backward(2)
 
     for r in (1, 2):
         send(give(2, r), 2, r, came(3, r))
         send(give(7, r), 7, r, came(6, r))
-    send(give(4, 0), 4, 0, mates(4))
-    send(give(5, 0), 5, 0, mates(5))
     send(give(2, 0), 2, 0, came(3, 0))
-
+    send(give(6, 0), 6, 0, came(5, 0))
     backward(RING)
     backward(1)
-    fill(1, 0)
+    send(give(7, 0), 7, 0, came(6, 0))
+    fill(1, 0, came(2, 0))
     go_if(not_first, give(1, 0))
     go_if(first, give_wrapped())
     for r in (1, 2):
@@ -362,7 +383,6 @@
         fill(RING, r, came(7, r))
         go_if(not_first, give(RING, r))
         go_if(first, gather(RING, r))
-    send(give(6, 0), 6, 0, came(4, 0), came(5, 0))
 
     @pl.when(first)
     def _():
@@ -390,7 +410,8 @@
 
         go(gather(0, r))
 
-    dq_t = mm(kt[...], p_buf[...]) * (inv * SCALE)
+    dq_t = mm(kt[:, near_part], p_buf[near_part, :]) * fade + mm(kt[:, far_part], p_buf[far_part, :])
+    dq_t = dq_t * (inv * SCALE)
     dq_ref[...] = jnp.concatenate([dq_t[:, i * HD:(i + 1) * HD].T for i in range(GROUP)], axis=1).astype(BF16)
     stores.append(store(1, dq_ref, dq_hbm))
 
@@ -406,8 +427,7 @@
         acc[0, z] = acc[0, z] + came(1, 0).astype(F32)
 
     own = acc[0, z]
-    for k in (2, 6, RING):
-        own = own + came(k, 0).astype(F32)
+    own = own + came(RING, 0).astype(F32)
     own = own + mates(0)
     dk_ref[...] = own[0].astype(BF16)
     dv_ref[...] = own[1].astype(BF16)
@@ -447,9 +467,9 @@
             vmem((N_HEAD, TOK, WIDTH), BF16),
             vmem((WIDTH, N_HEAD * WIDTH), BF16),
             vmem((HD, WIDTH), BF16),
-            vmem((WIDTH, HD), BF16),
+            vmem((2, WIDTH, HD), BF16),
             vmem((HD, WIDTH), BF16),
-            vmem((WIDTH, HD), BF16),
+            vmem((2, WIDTH, HD), BF16),
             vmem((RING + 1, BUNDLE, WIDTH), F32),
             vmem((keys, WIDTH), BF16),
             vmem((HD, keys), BF16),

time: 80.6 us -> 76.3 us (0.947)
  Pallas kernels: 79.3 us -> 75.5 us
    pallas_call x1, Pallas kernels: 77.5 us -> 73.7 us  [shards(): pl.pallas_call(kernel, out_shape=shapes, in_specs=[pl.BlockSpec(memory_sp...]
where the time goes in v4:
time: 76.3 us; the launch traced here: 76.1 us
  Pallas kernels  75.5 us (99%)
    pallas_call x1, Pallas kernels, shards(): pl.pallas_call(kernel, out_shape=shapes, in_specs=[pl.BlockSpec(memory_sp...  73.7 us
    pallas_call x1, Pallas kernels, shards(): pl.pallas_call(finish, out_shape=shapes, in_specs=[pl.BlockSpec(memory_sp...  1.75 us

profile of v4, /device:TPU:1, one launch (start us, length us, event | category | flops | bytes accessed | tf_op | source)
XLA Modules:
  0.0 76.1 jit_solution(4652943873246742544)
XLA Ops:
  0.6 73.7 %shard_map.101 = (bf16[128,384]{1,0:T(8,128)(2,1)}, bf16[128,384]{1,0:T(8,128)(2,1)}, bf16[128,384]{1,0:T(8,128)(2,1)}, bf16[128,128]{1,0:T(8,128)(2,1)}, bf16[128,128]{1,0:T(8,128)(2,1)}) custom-call(s32[8]{0:T(128)} %clip_ref.1, bf16[128,384]{1,0:T(8,128)(2,1)} %q_hbm.1, bf16[128,128]{1,0:T(8,128)(2,1)} %k_hbm.1, bf16[128,128]{1,0:T(8,128)(2,1)} %v_hbm.1, ...), custom_call_target="tpu_custom_call" | custom-call | flops 3000000000 | bytes 4000000 | tf_op jit(solution)/shard_map/pallas_call | solution.py:459
  74.4 1.7 %shard_map.102 = (bf16[128,384]{1,0:T(8,128)(2,1)}, bf16[128,384]{1,0:T(8,128)(2,1)}, bf16[128,384]{1,0:T(8,128)(2,1)}, bf16[128,128]{1,0:T(8,128)(2,1)}, bf16[128,128]{1,0:T(8,128)(2,1)}) custom-call(bf16[128,384]{1,0:T(8,128)(2,1)} %get-tuple-element.10.refs_0_, bf16[128,384]{1,0:T(8,128)(2,1)} %get-tuple-element.11.refs_1_, ...), custom_call_target="tpu_custom_call" | custom-call | tf_op jit(solution)/shard_map/pallas_call | solution.py:499

commit v5 on v4

--- a/solution.py
+++ b/solution.py
@@ -179,7 +179,6 @@
         at = part_of(k).start
         for i in range(LO):
             cols = slice(at + i * TOK, at + (i + 1) * TOK)
-            kt[:, cols] = kv[k, i, 0].T
             vt[:, cols] = kv[k, i, 1].T
 
     def og_up(d, early):
@@ -290,9 +289,6 @@
         m = lax.rem(hi + d, N_HI) * 2 + 1 - core
         part[m] = mm(attended, w[:, pl.ds(pl.multiple_of(m * WIDTH, HD), WIDTH)]).astype(BF16)
         go(part_copy(d))
-    for d in (1, 2, 3, 0):
-        m = lax.rem(hi + d, N_HI) * 2 + core
-        part[m] = mm(attended, w[:, pl.ds(pl.multiple_of(m * WIDTH, HD), WIDTH)]).astype(BF16)
     d_t = d_t.astype(F32)
     delta = jnp.sum(d_t * out_t, axis=0, keepdims=True)
     for i, factor in enumerate((inv * fade, inv)):
@@ -309,6 +305,7 @@
         for i in range(LO):
             acc[k, i, 0] = dk[i * TOK:(i + 1) * TOK, :]
             acc[k, i, 1] = dv[i * TOK:(i + 1) * TOK, :]
+            kt[:, rows.start + i * TOK:rows.start + (i + 1) * TOK] = kv[k, i, 0].T
         p_buf[rows, :] = ds
 
     back = [lax.rem(z + r, LO) for r in range(LO)]
@@ -348,6 +345,9 @@
     backward(5)
     for r in (1, 2):
         send(give(5, r), 5, r)
+    for d in (1, 2, 3, 0):
+        m = lax.rem(hi + d, N_HI) * 2 + core
+        part[m] = mm(attended, w[:, pl.ds(pl.multiple_of(m * WIDTH, HD), WIDTH)]).astype(BF16)
     for d in (1, 2, 3, 0):
         part_copy(d).wait_recv()
         m = lax.rem(hi + d, N_HI) * 2 + core
@@ -374,15 +374,15 @@
     send(give(6, 0), 6, 0, came(5, 0))
     backward(RING)
     backward(1)
+    for r in (1, 2):
+        send(give(1, r), 1, r, came(2, r))
+        fill(RING, r, came(7, r))
+        go_if(not_first, give(RING, r))
+        go_if(first, gather(RING, r))
     send(give(7, 0), 7, 0, came(6, 0))
     fill(1, 0, came(2, 0))
     go_if(not_first, give(1, 0))
     go_if(first, give_wrapped())
-    for r in (1, 2):
-        send(give(1, r), 1, r, came(2, r))
-        fill(RING, r, came(7, r))
-        go_if(not_first, give(RING, r))
-        go_if(first, gather(RING, r))
 
     @pl.when(first)
     def _():

time: 76.3 us -> 75.3 us (0.987)
  Pallas kernels: 75.5 us -> 74 us
    pallas_call x1, Pallas kernels: 73.7 us -> 72.3 us  [shards(): pl.pallas_call(kernel, out_shape=shapes, in_specs=[pl.BlockSpec(memory_sp...]
where the time goes in v5:
time: 75.3 us; the launch traced here: 74.6 us
  Pallas kernels  74 us (98%)
    pallas_call x1, Pallas kernels, shards(): pl.pallas_call(kernel, out_shape=shapes, in_specs=[pl.BlockSpec(memory_sp...  72.3 us
    pallas_call x1, Pallas kernels, shards(): pl.pallas_call(finish, out_shape=shapes, in_specs=[pl.BlockSpec(memory_sp...  1.75 us

profile of v5, /device:TPU:1, one launch (start us, length us, event | category | flops | bytes accessed | tf_op | source)
XLA Modules:
  0.0 74.6 jit_solution(15181800877757324013)
XLA Ops:
  0.6 72.3 %shard_map.101 = (bf16[128,384]{1,0:T(8,128)(2,1)}, bf16[128,384]{1,0:T(8,128)(2,1)}, bf16[128,384]{1,0:T(8,128)(2,1)}, bf16[128,128]{1,0:T(8,128)(2,1)}, bf16[128,128]{1,0:T(8,128)(2,1)}) custom-call(s32[8]{0:T(128)} %clip_ref.1, bf16[128,384]{1,0:T(8,128)(2,1)} %q_hbm.1, bf16[128,128]{1,0:T(8,128)(2,1)} %k_hbm.1, bf16[128,128]{1,0:T(8,128)(2,1)} %v_hbm.1, ...), custom_call_target="tpu_custom_call" | custom-call | flops 3000000000 | bytes 4000000 | tf_op jit(solution)/shard_map/pallas_call | solution.py:459
  72.9 1.7 %shard_map.102 = (bf16[128,384]{1,0:T(8,128)(2,1)}, bf16[128,384]{1,0:T(8,128)(2,1)}, bf16[128,384]{1,0:T(8,128)(2,1)}, bf16[128,128]{1,0:T(8,128)(2,1)}, bf16[128,128]{1,0:T(8,128)(2,1)}) custom-call(bf16[128,384]{1,0:T(8,128)(2,1)} %get-tuple-element.10.refs_0_, bf16[128,384]{1,0:T(8,128)(2,1)} %get-tuple-element.11.refs_1_, ...), custom_call_target="tpu_custom_call" | custom-call | tf_op jit(solution)/shard_map/pallas_call | solution.py:499

commit v6 on v5

--- a/solution.py
+++ b/solution.py
@@ -268,32 +268,14 @@
     inv = 1.0 / total
     out_t = near_out * fade + mm(vt[:, far_part], p_buf[far_part, :])
     out_t = (out_t * inv).astype(BF16).astype(F32)
-    attended = jnp.concatenate([out_t[:, i * HD:(i + 1) * HD].T for i in range(GROUP)], axis=1).astype(BF16)
-    att_ref[...] = attended
-
-    def store(i, src, dst):
-        c = pltpu.make_async_copy(src, dst, out_sem.at[i])
-        c.start()
-        return c
-
-    stores = [store(0, att_ref, att_hbm)]
-
-    def part_copy(d):
-        m = lax.rem(hi + d, N_HI) * 2 + 1 - core
-        return copy(part.at[m], psib.at[d], part_send.at[d], part_recv.at[d], sibling)
-
-    def far_copy(d):
-        return copy(pmine.at[d], pfar.at[d], pfar_send.at[d], pfar_recv.at[d], at_hi(d))
-
-    for d in (1, 2, 3, 0):
-        m = lax.rem(hi + d, N_HI) * 2 + 1 - core
-        part[m] = mm(attended, w[:, pl.ds(pl.multiple_of(m * WIDTH, HD), WIDTH)]).astype(BF16)
-        go(part_copy(d))
     d_t = d_t.astype(F32)
     delta = jnp.sum(d_t * out_t, axis=0, keepdims=True)
-    for i, factor in enumerate((inv * fade, inv)):
+
+    def scale_rows(i, factor):
         dos[i] = blocks_t(d_t * factor).astype(BF16)
         qs[i] = blocks_t(qt[...].astype(F32) * (factor * SCALE)).astype(BF16)
+
+    scale_rows(1, inv)
 
     def backward(k):
         rows, i = part_of(k), 1 if k in (4, 5) else 0
@@ -342,6 +324,27 @@
     backward(4)
     for r in (1, 2, 0):
         send(give(4, r), 4, r)
+    attended = jnp.concatenate([out_t[:, i * HD:(i + 1) * HD].T for i in range(GROUP)], axis=1).astype(BF16)
+    att_ref[...] = attended
+
+    def store(i, src, dst):
+        c = pltpu.make_async_copy(src, dst, out_sem.at[i])
+        c.start()
+        return c
+
+    stores = [store(0, att_ref, att_hbm)]
+
+    def part_copy(d):
+        m = lax.rem(hi + d, N_HI) * 2 + 1 - core
+        return copy(part.at[m], psib.at[d], part_send.at[d], part_recv.at[d], sibling)
+
+    def far_copy(d):
+        return copy(pmine.at[d], pfar.at[d], pfar_send.at[d], pfar_recv.at[d], at_hi(d))
+
+    for d in (1, 2, 3, 0):
+        m = lax.rem(hi + d, N_HI) * 2 + 1 - core
+        part[m] = mm(attended, w[:, pl.ds(pl.multiple_of(m * WIDTH, HD), WIDTH)]).astype(BF16)
+        go(part_copy(d))
     backward(5)
     for r in (1, 2):
         send(give(5, r), 5, r)
@@ -356,6 +359,7 @@
         if d:
             go(far_copy(d))
 
+    scale_rows(0, inv * fade)
     backward(3)
     backward(6)
 

time: 75.3 us -> 75.1 us (level)
  Pallas kernels: 74 us -> 73.1 us
    pallas_call x1, Pallas kernels: 72.3 us -> 71.4 us  [shards(): pl.pallas_call(kernel, out_shape=shapes, in_specs=[pl.BlockSpec(memory_sp...]
where the time goes in v6:
time: 75.1 us; the launch traced here: 73.8 us
  Pallas kernels  73.1 us (97%)
    pallas_call x1, Pallas kernels, shards(): pl.pallas_call(kernel, out_shape=shapes, in_specs=[pl.BlockSpec(memory_sp...  71.4 us
    pallas_call x1, Pallas kernels, shards(): pl.pallas_call(finish, out_shape=shapes, in_specs=[pl.BlockSpec(memory_sp...  1.75 us

profile of v6, /device:TPU:1, one launch (start us, length us, event | category | flops | bytes accessed | tf_op | source)
XLA Modules:
  0.0 73.8 jit_solution(1495391063106649405)
XLA Ops:
  0.6 71.4 %shard_map.101 = (bf16[128,384]{1,0:T(8,128)(2,1)}, bf16[128,384]{1,0:T(8,128)(2,1)}, bf16[128,384]{1,0:T(8,128)(2,1)}, bf16[128,128]{1,0:T(8,128)(2,1)}, bf16[128,128]{1,0:T(8,128)(2,1)}) custom-call(s32[8]{0:T(128)} %clip_ref.1, bf16[128,384]{1,0:T(8,128)(2,1)} %q_hbm.1, bf16[128,128]{1,0:T(8,128)(2,1)} %k_hbm.1, bf16[128,128]{1,0:T(8,128)(2,1)} %v_hbm.1, ...), custom_call_target="tpu_custom_call" | custom-call | flops 3000000000 | bytes 4000000 | tf_op jit(solution)/shard_map/pallas_call | solution.py:463
  72.0 1.7 %shard_map.102 = (bf16[128,384]{1,0:T(8,128)(2,1)}, bf16[128,384]{1,0:T(8,128)(2,1)}, bf16[128,384]{1,0:T(8,128)(2,1)}, bf16[128,128]{1,0:T(8,128)(2,1)}, bf16[128,128]{1,0:T(8,128)(2,1)}) custom-call(bf16[128,384]{1,0:T(8,128)(2,1)} %get-tuple-element.10.refs_0_, bf16[128,384]{1,0:T(8,128)(2,1)} %get-tuple-element.11.refs_1_, ...), custom_call_target="tpu_custom_call" | custom-call | tf_op jit(solution)/shard_map/pallas_call | solution.py:503
